TPU v7x, 32 devices: a whole 2x2x4 slice. The times are simulated.
32 devices in a mesh: tm: 8 (over z, y), zone: 4 (over x, core).
Axes of the slice: x: 2, y: 2, z: 4, core: 2. Of those that a mesh axis runs over, the one named last changes fastest.
Arguments:
- source_field: float32 [64, 8192], P('tm', 'zone'), may hold values from -6 to 6
- remap_weights: bfloat16 [64, 8, 128, 128], P('zone'), may hold values from -0.1875 to 0.1875
- block_columns: int32 [64, 8], P('zone'), may hold values from 0 to 63, all different within a row
- piece_sizes: int32 [4, 8], P('zone'), may hold values from 1 to 1024, 2048 in all within a row
- filter_taps: float32 [1023], replicated, may hold values from -0.1875 to 0.1875
Outputs:
- adjoint_field: float32 [64, 8192], P('tm', 'zone')
Inputs may be any that keep to these rules, and one draw needn't show every extreme that they name: `block_columns`: the 8 source blocks of one target block are distinct; every source block feeds some target block. `piece_sizes`: each row sums to 2048; its largest basin has exactly 1024 cells.
All inputs are finite; a program needn't handle non-finite values.
Results may differ from a plain program's by a relative error of at most 0.0038.
Values may be sent and summed in bfloat16 or wider, within the bound.
No kernel may reach another device: no remote copies, remote signals or barrier semaphores. Data moves between devices by JAX's collectives and lax.ppermute only.
A program may use at most 64 MiB of HBM per device.

v0:
```python
import jax
import jax.numpy as jnp
from jax import lax
from jax.sharding import PartitionSpec as P


def toeplitz_rows(filter_taps, block_rows, span):
    tap_count = filter_taps.shape[0]
    extended = jnp.concatenate([filter_taps, jnp.zeros((span + 1 - tap_count,), filter_taps.dtype)])
    flat = jnp.broadcast_to(extended[None, :], (block_rows, span + 1)).reshape(
        block_rows * (span + 1)
    )
    return flat[: block_rows * span].reshape(block_rows, span)


def banded(series, filter_taps):
    length, breadth = series.shape
    tap_count = filter_taps.shape[0]
    half_width = (tap_count - 1) // 2
    block_rows = min(512, length)
    toeplitz = toeplitz_rows(filter_taps, block_rows, block_rows + 2 * half_width)
    padded = jnp.pad(series, ((half_width, half_width), (0, 0)))

    def one_block(start):
        window = lax.dynamic_slice_in_dim(padded, start, block_rows + 2 * half_width, 0)
        return jnp.dot(
            toeplitz, window, precision=lax.Precision.HIGHEST, preferred_element_type=jnp.float32
        )

    starts = jnp.arange(length // block_rows) * block_rows
    return lax.map(one_block, starts).reshape(length, breadth)


def relayout(sendbuf, filter_taps):
    received = lax.all_to_all(sendbuf, "tm", split_axis=1, concat_axis=0, tiled=True)
    total_rows, single, breadth = received.shape
    result = banded(received.reshape(total_rows, breadth), filter_taps).reshape(
        total_rows, single, breadth
    )
    return lax.all_to_all(
        result.astype(jnp.bfloat16), "tm", split_axis=0, concat_axis=1, tiled=True
    ).astype(result.dtype)


def shards(source_field, remap_weights, block_columns, piece_sizes, filter_taps):
    local_rows, zone_cells = source_field.shape
    owners = lax.axis_size("tm")
    block_size = remap_weights.shape[2]
    zone_blocks = remap_weights.shape[0]
    all_blocks = zone_blocks * lax.axis_size("zone")
    xlow = source_field.astype(jnp.bfloat16)
    xwhole = lax.all_gather(xlow, "zone", axis=1, tiled=True)
    picked = xwhole.reshape(local_rows, all_blocks, block_size)[:, block_columns]
    wind = jnp.einsum("tikb,ikab->tia", picked, remap_weights, preferred_element_type=jnp.float32)
    wind = wind.reshape(local_rows, zone_cells)
    stress = wind * jnp.abs(wind)
    sizes_row = piece_sizes[0]
    ends = jnp.cumsum(sizes_row)
    begins = ends - sizes_row
    cell_ids = jnp.arange(zone_cells, dtype=jnp.int32)
    member_mask = (cell_ids[:, None] >= begins[None, :]) & (cell_ids[:, None] < ends[None, :])
    member = member_mask.astype(jnp.float32)
    totals = jnp.dot(stress, member, precision=lax.Precision.HIGHEST)
    means = totals / sizes_row.astype(jnp.float32)[None, :]
    anomaly = stress - jnp.dot(means, member.T, precision=lax.Precision.HIGHEST)
    sendbuf = anomaly.reshape(local_rows, owners, zone_cells // owners)
    filtered = relayout(sendbuf, filter_taps).reshape(local_rows, zone_cells)
    flow_low = filtered.astype(jnp.bfloat16).reshape(local_rows, zone_blocks, block_size)
    contrib = jnp.einsum(
        "tia,ikab->tikb", flow_low, remap_weights, preferred_element_type=jnp.float32
    )
    partial_sum = jnp.zeros((local_rows, all_blocks, block_size), jnp.float32)
    partial_sum = partial_sum.at[:, block_columns].add(contrib)
    partial_sum = partial_sum.reshape(local_rows, all_blocks * block_size)
    return lax.psum_scatter(partial_sum, "zone", scatter_dimension=1, tiled=True)


def solution(mesh):
    return jax.shard_map(
        shards,
        mesh=mesh,
        in_specs=(
            P("tm", "zone"),
            P("zone", None, None, None),
            P("zone", None),
            P("zone", None),
            P(),
        ),
        out_specs=P("tm", "zone"),
        check_vma=False,
    )
```

profile of v0, /device:TPU:0, one launch (start us, length us, event | category | flops | bytes accessed | tf_op | source)
XLA Modules:
  0.0 79.0 jit_solution(8890200508260986181)
XLA Ops:
  6.5 0.8 %reduce-window.4 = s32[8,1]{0,1:T(1,128)S(1)} reduce-window(s32[8,1]{0,1:T(1,128)} %bitcast.59, s32[]{:T(128)} %constant.10.clone.1), window={size=8x1 pad=7_0x0_0}, to_apply=%region_0.0 | reduce-window | flops 56 | bytes 68 | tf_op jit(solution)/shard_map/reduce-window
  7.4 0.7 convert_bitcast_fusion
  8.1 0.7 compare_select_fusion
  8.8 0.1 copy.10
  8.9 0.1 reshape.58
  9.0 0.8 %convert_element_type.21 = bf16[8,2048]{1,0:T(8,128)(2,1)S(1)} convert(f32[8,2048]{1,0:T(8,128)} %param.5) | non-fusion elementwise | flops 16384 | bytes 98304 | tf_op jit(solution)/shard_map/convert_element_type | solution.py:51
  9.8 6.5 %all_gather.3 = bf16[8,8192]{1,0:T(8,128)(2,1)S(1)} all-gather(bf16[8,2048]{1,0:T(8,128)(2,1)S(1)} %convert_element_type.21), channel_id=1, replica_groups=mesh['tm'=8,'zone'=4] {'zone'}, dimensions={1}, use_global_device_ids=true | all-gather | bytes 163840 | tf_op jit(solution)/shard_map/all_gather | solution.py:52
  16.3 0.7 gather_fusion
  17.0 3.4 %abs_multiply_fusion = f32[8,2048]{1,0:T(8,128)S(1)} fusion(bf16[8,16,8,128]{3,0,2,1:T(8,128)(2,1)S(1)} %bitcast.56, bf16[16,8,128,128]{3,2,1,0:T(8,128)(2,1)} %param.6), kind=kOutput, calls=%fused_computation.15 | convolution fusion | flops 33587200 | bytes 4521984 | tf_op jit(solution)/shard_map/tikb,ikab->tia/dot_general | solution.py:54
  20.4 0.5 convolution_divide_fusion
  20.9 1.3 %convolution_subtract_fusion = f32[8,2048]{1,0:T(8,128)} fusion(f32[8,2048]{1,0:T(8,128)S(1)} %abs_multiply_fusion, f32[8,8]{1,0:T(8,128)S(1)} %convolution_divide_fusion, s32[8]{0:T(128)S(1)} %bitcast.61, s32[8]{0:T(128)S(1)} %get-tuple-element.16), kind=kOutput, calls=%fused_computation.2 | convolution fusion | flops 1638400 | bytes 131392 | tf_op jit(solution)/shard_map/dot_general | solution.py:65
  22.2 6.2 %all-to-all-start = ((f32[8,8,256]{2,0,1:T(8,128)}), f32[8,8,256]{2,0,1:T(8,128)S(1)}, u32[]{:S(2)}, u32[]{:S(2)}) async-start(f32[8,8,256]{2,0,1:T(8,128)} %bitcast.14), calls=%async_computation | async-start | bytes 131072 | tf_op jit(solution)/shard_map/all_to_all | solution.py:35
  28.4 0.0 reduce-scatter.2.cloned.1.call-start
  28.5 0.2 reshape.39
  28.7 0.3 reshape.40
  29.0 6.3 %all-to-all-done = f32[8,8,256]{2,0,1:T(8,128)S(1)} async-done(((f32[8,8,256]{2,0,1:T(8,128)}), f32[8,8,256]{2,0,1:T(8,128)S(1)}, u32[]{:S(2)}, u32[]{:S(2)}) %all-to-all-start) | async-done | bytes 65568 | tf_op jit(solution)/shard_map/all_to_all | solution.py:35
  35.3 0.4 fusion.1
  35.8 0.5 broadcast.19
  36.3 0.7 reduce
  37.0 9.1 %all_to_all.33 = bf16[8,2,1024]{2,1,0:T(2,128)(2,1)S(1)} all-to-all(bf16[8,2,1024]{2,1,0:T(2,128)(2,1)S(1)} %reshape.70), channel_id=1, replica_groups=mesh['tm'=8,'zone'=4] {'tm'}, dimensions={0} | all-to-all | bytes 65536 | tf_op jit(solution)/shard_map/all_to_all | solution.py:40
  46.1 2.8 %fusion.13 = f32[16,8,8,128]{3,1,2,0:T(8,128)S(1)} fusion(bf16[8,16,128,1]{2,0,3,1:T(8,128)(2,1)S(1)} %bitcast.58, bf16[16,8,128,128]{3,2,1,0:T(8,128)(2,1)} %param.6), kind=kOutput, calls=%fused_computation.22 | convolution fusion | flops 33554432 | bytes 4751360 | tf_op jit(solution)/shard_map/tia,ikab->tikb/dot_general | solution.py:69
  48.9 4.9 %scatter_fusion = f32[8,64,128]{2,0,1:T(8,128)S(1)} fusion(f32[8,64,128]{2,0,1:T(8,128)S(1)} %broadcast_in_dim.8, s32[128]{0:T(128)S(1)} %reshape.58, f32[128,8,128]{2,1,0:T(8,128)S(1)} %bitcast.53), kind=kCustom, calls=%fused_computation.1 | custom fusion | flops 131072 | bytes 1573376 | tf_op jit(solution)/shard_map/scatter-add | solution.py:73
  53.9 0.7 copy-done
  54.6 17.6 %reduce-scatter.2.cloned.1.call-done = f32[8,2048]{1,0:T(8,128)} async-done(((f32[8,8192]{1,0:T(8,128)}), f32[8,2048]{1,0:T(8,128)}) %reduce-scatter.2.cloned.1.call-update) | async-done | bytes 65552 | tf_op jit(solution)/shard_map/reduce_scatter | solution.py:75
  (11 shorter events, 0.1 us)
Async XLA Ops:
  6.5 21.9 %copy-start.1 = (f32[1023]{0:T(1024)S(1)}, f32[1023]{0:T(1024)}, u32[]{:S(2)}) copy-start(f32[1023]{0:T(1024)} %param.9) | copy-start | bytes 12280
  22.2 13.1 %all-to-all-start = ((f32[8,8,256]{2,0,1:T(8,128)}), f32[8,8,256]{2,0,1:T(8,128)S(1)}, u32[]{:S(2)}, u32[]{:S(2)}) async-start(f32[8,8,256]{2,0,1:T(8,128)} %bitcast.14), calls=%async_computation | async-start | bytes 131072 | tf_op jit(solution)/shard_map/all_to_all | solution.py:35
  28.4 43.7 %reduce-scatter.2.cloned.1.call-start = ((), (), s32[]{:S(2)}) async-start(), calls=%async_computation.3 | async-start | bytes 327680 | tf_op jit(solution)/shard_map/reduce_scatter | solution.py:75
  53.9 0.7 copy-start
Sparse Core Ops, SparseCore 0:
  54.7 17.3 reduce-scatter.1
where the time goes:
time: 79.4 us; the launch traced here: 79 us
  waiting for transfers between devices  23.9 us (30%)
  blocking collectives  15.5 us (20%)
  between operations  13.5 us (17%)
  other arithmetic  8.7 us (11%)
  matrix products  8.47 us (11%)
  starting transfers between devices  6.26 us (8%)
  local copies, waits for them, and re-layouts  2.63 us (3%)
    reduce_scatter x1, waiting for transfers between devices, shards(): lax.psum_scatter(partial_sum, 'zone', scatter_dimension=1, tiled=True)  17.6 us
    all_to_all x1, blocking collectives, relayout(): lax.all_to_all(result.astype(jnp.bfloat16), 'tm', split_axis=0, concat_ax...  9.06 us
    all_gather x1, blocking collectives, shards(): xwhole = lax.all_gather(xlow, 'zone', axis=1, tiled=True)  6.47 us
    all_to_all x1, waiting for transfers between devices, relayout(): lax.all_to_all(sendbuf, 'tm', split_axis=1, concat_axis=0, tiled=True)  6.33 us
    all_to_all x1, starting transfers between devices, relayout(): lax.all_to_all(sendbuf, 'tm', split_axis=1, concat_axis=0, tiled=True)  6.23 us
    scatter-add x1, other arithmetic, shards(): partial_sum = partial_sum.at[:, block_columns].add(contrib)  4.93 us
    dot_general x1, matrix products, shards(): jnp.einsum('tikb,ikab->tia', picked, remap_weights, preferred_element_typ...  3.37 us
    dot_general x1, matrix products, shards(): jnp.einsum('tia,ikab->tikb', flow_low, remap_weights, preferred_element_t...  2.84 us
  transfers between devices with their start and end apart: 2, of which 2 were waited for; matrix products, arithmetic and copies ran while one was open for 1% of the time, Pallas kernels for 0%

commit v1 on v0

v1 whole, which is shorter than its diff:
```python
import functools
import jax
import jax.numpy as jnp
from jax import lax
from jax.experimental import pallas as pl
from jax.experimental.pallas import tpu as pltpu
from jax.sharding import PartitionSpec as P

VMEM = pl.BlockSpec(memory_space=pltpu.VMEM)
SMEM = pl.BlockSpec(memory_space=pltpu.SMEM)
HBM = pl.BlockSpec(memory_space=pltpu.HBM)
NT = (((1,), (1,)), ((), ()))
LIMIT = 16 * 2**20
DIRECT = 8
NEAR = 4


def three_parts(value):
    high = value.astype(jnp.bfloat16)
    rest = value - high.astype(jnp.float32)
    middle = rest.astype(jnp.bfloat16)
    low = (rest - middle.astype(jnp.float32)).astype(jnp.bfloat16)
    return high, middle, low


def ahead(snapshots, half_width, width):
    return -(-max(0, snapshots + width - half_width) // 128) * 128


def prepare_kernel(where_ref, sizes_hbm, taps_hbm, weights_ref, *refs):
    held_ref, rows_ref, member_ref, count_ref, line_ref, sizes_ref, taps_ref, sems = refs
    taps_total = taps_hbm.shape[1]
    parts = sems.shape[0] - 2
    taps_copy = pltpu.make_async_copy(taps_hbm, taps_ref, sems.at[parts])
    sizes_copy = pltpu.make_async_copy(sizes_hbm, sizes_ref, sems.at[parts + 1])
    taps_copy.start()
    sizes_copy.start()
    each = weights_ref.shape[0] // parts
    copies = [
        pltpu.make_async_copy(
            weights_ref.at[pl.ds(n * each, each)], held_ref.at[pl.ds(n * each, each)], sems.at[n]
        )
        for n in range(parts)
    ]
    for copy in copies:
        copy.start()

    rows, width = line_ref.shape
    half_width = (taps_total - 1) // 2
    steps = rows_ref.shape[0] // rows
    before = ahead(steps * rows_ref.shape[1], half_width, rows_ref.shape[1])
    line_ref[...] = jnp.zeros_like(line_ref)
    taps_copy.wait()
    line_ref[:, before : before + taps_total] = jnp.broadcast_to(
        taps_ref[...], (rows, taps_total)
    )
    line = line_ref[...]
    row_ids = lax.broadcasted_iota(jnp.int32, (rows, 1), 0)
    slanted = line
    for r in range(1, rows):
        slanted = jnp.where(row_ids == r, pltpu.roll(line, r, 1), slanted)
    line_ref[...] = slanted
    near = rows_ref.shape[1] // rows
    lanes = lax.broadcasted_iota(jnp.int32, (rows, near * rows), 1)
    at = where_ref[1]
    for step in range(steps):
        target = at ^ (near * step) if steps <= DIRECT else near * step + (at & (near - 1))
        found = jnp.zeros((rows, near * rows), jnp.float32)
        for n in range(near):
            base = ((at ^ n) - target) * rows + half_width - n * rows + before
            first = pl.multiple_of((base >> 7) << 7, 128)
            window = line_ref[:, pl.ds(first, 256)]
            turned = pltpu.roll(window, (256 - (base & 127)) & 255, 1)
            found = jnp.where(lanes >= n * rows, turned[:, : near * rows], found)
        rows_ref[step * rows : (step + 1) * rows, :] = found

    sizes_copy.wait()
    basins, cells = member_ref.shape
    cell_ids = lax.broadcasted_iota(jnp.int32, (1, cells), 1)
    basin_ids = jnp.zeros((1, cells), jnp.int32)
    basin_lanes = lax.broadcasted_iota(jnp.int32, (1, basins), 1)
    counts = jnp.zeros((1, basins), jnp.int32)
    end = 0
    for g in range(basins):
        counts = jnp.where(basin_lanes == g, sizes_ref[0, g], counts)
        if g:
            basin_ids += (cell_ids >= end).astype(jnp.int32)
        end = end + sizes_ref[0, g]
    member = lax.broadcasted_iota(jnp.int32, (basins, cells), 0) == basin_ids
    member_ref[...] = member.astype(jnp.float32).astype(jnp.bfloat16)
    count_ref[...] = counts.astype(jnp.float32)
    for copy in copies:
        copy.wait()


def prepare(where, sizes, filter_taps, weights, steps, near, rows):
    taps_total = filter_taps.shape[0]
    half_width = (taps_total - 1) // 2
    snapshots = near * steps * rows
    width = ahead(snapshots, half_width, near * rows) + max(taps_total + rows, half_width + snapshots) + 256
    width = -(-width // 128) * 128
    basins = sizes.shape[1]
    cells = weights.shape[0] * weights.shape[2]
    return pl.pallas_call(
        prepare_kernel,
        out_shape=[
            jax.ShapeDtypeStruct(weights.shape, weights.dtype),
            jax.ShapeDtypeStruct((steps * rows, near * rows), jnp.float32),
            jax.ShapeDtypeStruct((basins, cells), jnp.bfloat16),
            jax.ShapeDtypeStruct((1, basins), jnp.float32),
        ],
        in_specs=[SMEM, HBM, HBM, HBM],
        out_specs=[VMEM] * 4,
        scratch_shapes=[
            pltpu.VMEM((rows, width), jnp.float32),
            pltpu.SMEM(sizes.shape, sizes.dtype),
            pltpu.VMEM((1, taps_total), jnp.float32),
            pltpu.SemaphoreType.DMA((6,)),
        ],
        compiler_params=pltpu.CompilerParams(vmem_limit_bytes=46 * 2**20),
        cost_estimate=pl.CostEstimate(flops=0, bytes_accessed=8 * 2**20, transcendentals=0),
        name="prepare",
    )(where, sizes, filter_taps.reshape(1, -1), weights)


def remap_kernel(zones, where_ref, columns_ref, member_ref, count_ref, *refs):
    x_refs, (weights_ref, *refs) = refs[:zones], refs[zones:]
    c_refs, (blocks_ref, total_ref) = refs[:zones], refs[zones:]
    zone_blocks, slots, size, _ = weights_ref.shape
    rows = x_refs[0].shape[0]
    me = where_ref[0]
    for step in range(zones):
        first = (me ^ step) * zone_blocks
        for b in range(zone_blocks):
            blocks_ref[first + b] = x_refs[step][:, b * size : (b + 1) * size].astype(jnp.float32)
    total_ref[...] = jnp.zeros_like(total_ref)

    pieces = []
    for i in range(zone_blocks):
        picked = jnp.concatenate([blocks_ref[columns_ref[k, i]] for k in range(slots)], axis=1)
        wide = jnp.concatenate([weights_ref[i, k] for k in range(slots)], axis=1)
        wind = lax.dot_general(
            picked.astype(jnp.bfloat16), wide, NT, preferred_element_type=jnp.float32
        )
        pieces.append(wind * jnp.abs(wind))
    stress = jnp.concatenate(pieces, axis=1)

    member = member_ref[...]
    parts = lax.dot_general(
        jnp.concatenate(three_parts(stress), axis=0), member, NT, preferred_element_type=jnp.float32
    )
    totals = parts[:rows] + parts[rows : 2 * rows] + parts[2 * rows :]
    means = totals / count_ref[...]
    spread = jnp.dot(
        jnp.concatenate(three_parts(means), axis=0), member, preferred_element_type=jnp.float32
    )
    anomaly = stress - (spread[:rows] + spread[rows : 2 * rows] + spread[2 * rows :])

    high = anomaly.astype(jnp.bfloat16)
    low = (anomaly - high.astype(jnp.float32)).astype(jnp.bfloat16)
    both = jnp.concatenate([high, low], axis=0)
    for i in range(zone_blocks):
        wide = jnp.concatenate([weights_ref[i, k] for k in range(slots)], axis=1)
        back = jnp.dot(
            both[:, i * size : (i + 1) * size], wide, preferred_element_type=jnp.float32
        )
        back = back[:rows] + back[rows:]
        for k in range(slots):
            column = columns_ref[k, i]
            total_ref[column] += back[:, k * size : (k + 1) * size]
    for step in range(zones):
        first = (me ^ step) * zone_blocks
        for b in range(zone_blocks):
            c_refs[step][:, b * size : (b + 1) * size] = total_ref[first + b].astype(
                c_refs[step].dtype
            )


def remap(where, columns, member, counts, xs, weights):
    zones = len(xs)
    rows, cells = xs[0].shape
    all_blocks = zones * weights.shape[0]
    size = weights.shape[2]
    outs = [
        jax.ShapeDtypeStruct((rows, cells), jnp.bfloat16 if step else jnp.float32)
        for step in range(zones)
    ]
    return pl.pallas_call(
        functools.partial(remap_kernel, zones),
        out_shape=outs,
        in_specs=[SMEM, SMEM] + [VMEM] * (3 + zones),
        out_specs=[VMEM] * zones,
        scratch_shapes=[
            pltpu.VMEM((all_blocks, rows, size), jnp.float32),
            pltpu.VMEM((all_blocks, rows, size), jnp.float32),
        ],
        compiler_params=pltpu.CompilerParams(vmem_limit_bytes=LIMIT),
        cost_estimate=pl.CostEstimate(flops=10**8, bytes_accessed=8 * 2**20, transcendentals=0),
        name="remap",
    )(where, columns, member, counts, *xs, weights)


def gather_kernel(*refs):
    *parts, total_ref, low_ref = refs
    total = sum(r[...].astype(jnp.float32) for r in parts)
    total_ref[...] = total
    low_ref[...] = total.astype(low_ref.dtype)


def add_zones(parts):
    return pl.pallas_call(
        gather_kernel,
        out_shape=[jax.ShapeDtypeStruct(parts[0].shape, d) for d in (jnp.float32, jnp.bfloat16)],
        in_specs=[VMEM] * len(parts),
        out_specs=[VMEM] * 2,
        compiler_params=pltpu.CompilerParams(vmem_limit_bytes=LIMIT),
        name="add_zones",
    )(*parts)


def filter_kernel(near, taps_ref, *refs):
    values, outs = refs[:near], refs[near:]
    rows = values[0].shape[0]
    together = jnp.concatenate([r[...].astype(jnp.float32) for r in values], axis=0)
    result = jnp.dot(
        taps_ref[...], together, precision=lax.Precision.HIGHEST, preferred_element_type=jnp.float32
    )
    if len(outs) == 1:
        outs[0][...] = result.astype(outs[0].dtype)
        return
    for step, out in enumerate(outs):
        out[...] = result[step * rows : (step + 1) * rows].astype(out.dtype)


def time_filter(taps, values):
    rows, cells = values[0].shape
    steps = taps.shape[0] // rows
    if steps <= DIRECT:
        outs = [
            jax.ShapeDtypeStruct((rows, cells), jnp.bfloat16 if step else jnp.float32)
            for step in range(steps)
        ]
    else:
        outs = [jax.ShapeDtypeStruct((steps * rows, cells), jnp.bfloat16)]
    return pl.pallas_call(
        functools.partial(filter_kernel, len(values)),
        out_shape=outs,
        in_specs=[VMEM] * (1 + len(values)),
        out_specs=[VMEM] * len(outs),
        compiler_params=pltpu.CompilerParams(vmem_limit_bytes=LIMIT),
        name="time_filter",
    )(taps, *values)


def sum_kernel(*refs):
    refs[-1][...] = sum(r[...].astype(jnp.float32) for r in refs[:-1])


def add_up(parts):
    return pl.pallas_call(
        sum_kernel,
        out_shape=jax.ShapeDtypeStruct(parts[0].shape, jnp.float32),
        in_specs=[VMEM] * len(parts),
        out_specs=VMEM,
        compiler_params=pltpu.CompilerParams(vmem_limit_bytes=LIMIT),
        name="add_up",
    )(*parts)


def swap(value, axis, by):
    return lax.ppermute(value, axis, [(i, i ^ by) for i in range(lax.axis_size(axis))])


def shards(source_field, remap_weights, block_columns, piece_sizes, filter_taps):
    rows, cells = source_field.shape
    zones, owners = lax.axis_size("zone"), lax.axis_size("tm")
    near = min(NEAR, owners)
    steps = owners // near
    where = jnp.stack([lax.axis_index("zone"), lax.axis_index("tm")])
    xlow = source_field.astype(jnp.bfloat16)
    xs = [xlow] + [swap(xlow, "zone", step) for step in range(1, zones)]
    held, taps, member, counts = prepare(
        where, piece_sizes, filter_taps, remap_weights, steps, near, rows
    )
    sent = remap(where, block_columns.T, member, counts, xs, held)

    summed, low = add_zones(
        [sent[0]] + [swap(sent[step], "zone", step) for step in range(1, zones)]
    )
    parts = time_filter(taps, [summed] + [swap(low, "tm", n) for n in range(1, near)])
    if steps <= DIRECT:
        last = [parts[0]] + [swap(parts[step], "tm", near * step) for step in range(1, steps)]
        return add_up(last)
    groups = [list(range(side, owners, near)) for side in range(near)]
    parts = lax.all_to_all(
        parts[0].reshape(steps, rows, cells), "tm", 0, 0, axis_index_groups=groups
    )
    return parts.astype(jnp.float32).sum(axis=0)


def solution(mesh):
    return jax.shard_map(
        shards,
        mesh=mesh,
        in_specs=(
            P("tm", "zone"),
            P("zone", None, None, None),
            P("zone", None),
            P("zone", None),
            P(),
        ),
        out_specs=P("tm", "zone"),
        check_vma=False,
    )
```

time: 79.4 us -> 29.3 us (0.37)
  blocking collectives: 15.5 us -> 0 us
  waiting for transfers between devices: 23.9 us -> 8.95 us
  between operations: 13.5 us -> 0.06 us
  matrix products: 8.47 us -> 0 us
  other arithmetic: 8.7 us -> 0.93 us
  Pallas kernels: 0 us -> 6.5 us
  starting transfers between devices: 6.26 us -> 11.2 us
  local copies, waits for them, and re-layouts: 2.63 us -> 1.34 us
    reduce_scatter x1 -> x0, waiting for transfers between devices: 17.6 us -> none  [shards(): lax.psum_scatter(partial_sum, 'zone', scatter_dimension=1, tiled=True)]
    ppermute x0 -> x10, starting transfers between devices: none -> 11.2 us  [swap(): lax.ppermute(value, axis, [(i, i ^ by) for i in range(lax.axis_size(axis))])]
    all_to_all x1 -> x0, blocking collectives: 9.06 us -> none  [relayout(): lax.all_to_all(result.astype(jnp.bfloat16), 'tm', split_axis=0, concat_ax...]
    ppermute x0 -> x10, waiting for transfers between devices: none -> 8.95 us  [swap(): lax.ppermute(value, axis, [(i, i ^ by) for i in range(lax.axis_size(axis))])]
    dot_general x5 -> x0, matrix products: 8.47 us -> none  [the longest x1 3.37 us: shards(): jnp.einsum('tikb,ikab->tia', picked, remap_weights, preferred_element_typ...]
    pallas_call x0 -> x5, Pallas kernels: none -> 6.5 us  [the longest x1 2.79 us: remap(): pl.pallas_call(functools.partial(remap_kernel, zones), out_shape=outs, in...]
    all_gather x1 -> x0, blocking collectives: 6.47 us -> none  [shards(): xwhole = lax.all_gather(xlow, 'zone', axis=1, tiled=True)]
    all_to_all x1 -> x0, waiting for transfers between devices: 6.33 us -> none  [relayout(): lax.all_to_all(sendbuf, 'tm', split_axis=1, concat_axis=0, tiled=True)]
  transfers between devices with their start and end apart: 2 -> 10, of which waited for: 2 -> 6; matrix products, arithmetic and copies ran while one was open for 1% -> 0% of each run, Pallas kernels for 0% -> 10%
where the time goes in v1:
time: 29.3 us; the launch traced here: 29 us
  starting transfers between devices  11.2 us (38%)
  waiting for transfers between devices  8.95 us (31%)
  Pallas kernels  6.5 us (22%)
  local copies, waits for them, and re-layouts  1.34 us (5%)
  other arithmetic  0.93 us (3%)
    ppermute x10, starting transfers between devices, swap(): lax.ppermute(value, axis, [(i, i ^ by) for i in range(lax.axis_size(axis))])  11.2 us
    ppermute x10, waiting for transfers between devices, swap(): lax.ppermute(value, axis, [(i, i ^ by) for i in range(lax.axis_size(axis))])  8.95 us
    pallas_call x1, Pallas kernels, remap(): pl.pallas_call(functools.partial(remap_kernel, zones), out_shape=outs, in...  2.79 us
    pallas_call x1, Pallas kernels, prepare(): pl.pallas_call(prepare_kernel, out_shape=[jax.ShapeDtypeStruct(weights.sh...  2.77 us
    unnamed x6, local copies, waits for them, and re-layouts  1.34 us
    convert_element_type x1, other arithmetic, shards(): xlow = source_field.astype(jnp.bfloat16)  0.86 us
    pallas_call x1, Pallas kernels, add_up(): pl.pallas_call(sum_kernel, out_shape=jax.ShapeDtypeStruct(parts[0].shape,...  0.64 us
  transfers between devices with their start and end apart: 10, of which 6 were waited for; matrix products, arithmetic and copies ran while one was open for 0% of the time, Pallas kernels for 10%

profile of v1, /device:TPU:0, one launch (start us, length us, event | category | flops | bytes accessed | tf_op | source)
XLA Modules:
  0.0 29.0 jit_solution(10778543609719318057)
XLA Ops:
  0.0 0.9 %convert_element_type.3.refs_0_ = bf16[8,2048]{1,0:T(8,128)(2,1)S(1)} convert(f32[8,2048]{1,0:T(8,128)} %param.5) | non-fusion elementwise | flops 16384 | bytes 98304 | tf_op jit(solution)/shard_map/convert_element_type | solution.py:280
  0.9 2.4 %collective-permute-start.2 = (bf16[8,2048]{1,0:T(8,128)(2,1)S(1)}, bf16[8,2048]{1,0:T(8,128)(2,1)S(1)}, u32[]{:S(2)}, u32[]{:S(2)}) collective-permute-start(bf16[8,2048]{1,0:T(8,128)(2,1)S(1)} %convert_element_type.3.refs_0_), channel_id=1, source_target_pairs={{0,3},{1,2},{2,1},{3,0},{4,7},{5,6},{6,5},{7,4},{8,11},{9,10},{10,... | collective-permute-start | bytes 98312 | tf_op jit(solution)/shard_map/ppermute | solution.py:271
  3.2 0.6 %collective-permute-start.1 = (bf16[8,2048]{1,0:T(8,128)(2,1)S(1)}, bf16[8,2048]{1,0:T(8,128)(2,1)S(1)}, u32[]{:S(2)}, u32[]{:S(2)}) collective-permute-start(bf16[8,2048]{1,0:T(8,128)(2,1)S(1)} %convert_element_type.3.refs_0_), channel_id=1, source_target_pairs={{0,2},{1,3},{2,0},{3,1},{4,6},{5,7},{6,4},{7,5},{8,10},{9,11},{10,... | collective-permute-start | bytes 98312 | tf_op jit(solution)/shard_map/ppermute | solution.py:271
  3.8 0.1 collective-permute-start
  3.9 0.1 pad_add_fusion.where_ref
  4.0 0.7 %copy-done = f32[1023]{0:T(1024)S(1)} copy-done((f32[1023]{0:T(1024)S(1)}, f32[1023]{0:T(1024)}, u32[]{:S(2)}) %copy-start) | copy-done | bytes 4116
  4.7 0.7 %copy-done.2 = s32[1,8]{1,0:T(1,128)S(1)} copy-done((s32[1,8]{1,0:T(1,128)S(1)}, s32[1,8]{1,0:T(1,128)}, u32[]{:S(2)}) %copy-start.2) | copy-done | bytes 56
  5.3 2.8 %prepare.1 = (bf16[16,8,128,128]{3,2,1,0:T(8,128)(2,1)S(1)}, f32[16,32]{1,0:T(8,128)S(1)}, bf16[8,2048]{1,0:T(8,128)(2,1)S(1)}, f32[1,8]{1,0:T(1,128)S(1)}) custom-call(s32[2]{0:T(128)S(1)} %pad_add_fusion.where_ref, s32[1,8]{1,0:T(1,128)S(1)} %copy-done.2, f32[1,1023]{1,0:T(1,128)S(1)} %bitcast.4, bf16[16,8,128,128]{3,2,1,0:T(8,128)(2,1)} %weights_ref.1), custom_call_target="tpu_custom_call" | custom-call | bytes 8388608 | tf_op jit(solution)/shard_map/prepare/pallas_call | solution.py:104
  8.2 2.8 %remap.1 = (f32[8,2048]{1,0:T(8,128)S(1)}, bf16[8,2048]{1,0:T(8,128)(2,1)S(1)}, bf16[8,2048]{1,0:T(8,128)(2,1)S(1)}, bf16[8,2048]{1,0:T(8,128)(2,1)S(1)}) custom-call(s32[2]{0:T(128)S(1)} %pad_add_fusion.where_ref, s32[8,16]{1,0:T(8,128)S(1)} %bitcast.5, bf16[8,2048]{1,0:T(8,128)(2,1)S(1)} %get-tuple-element.18.member_ref, ...), custom_call_target="tpu_custom_call" | custom-call | flops 100000000 | bytes 8388608 | tf_op jit(solution)/shard_map/remap/pallas_call | solution.py:188
  11.0 0.5 %collective-permute-start.3 = (bf16[8,2048]{1,0:T(8,128)(2,1)S(1)}, bf16[8,2048]{1,0:T(8,128)(2,1)S(1)}, u32[]{:S(2)}, u32[]{:S(2)}) collective-permute-start(bf16[8,2048]{1,0:T(8,128)(2,1)S(1)} %get-tuple-element.22), channel_id=1, source_target_pairs={{0,1},{1,0},{2,3},{3,2},{4,5},{5,4},{6,7},{7,6},{8,9},{9,8},{10,11... | collective-permute-start | bytes 98312 | tf_op jit(solution)/shard_map/ppermute | solution.py:271
  11.4 1.4 %collective-permute-start.4 = (bf16[8,2048]{1,0:T(8,128)(2,1)S(1)}, bf16[8,2048]{1,0:T(8,128)(2,1)S(1)}, u32[]{:S(2)}, u32[]{:S(2)}) collective-permute-start(bf16[8,2048]{1,0:T(8,128)(2,1)S(1)} %get-tuple-element.23), channel_id=1, source_target_pairs={{0,2},{1,3},{2,0},{3,1},{4,6},{5,7},{6,4},{7,5},{8,10},{9,11},{10,... | collective-permute-start | bytes 98312 | tf_op jit(solution)/shard_map/ppermute | solution.py:271
  12.9 0.1 collective-permute-start.5
  12.9 2.4 %collective-permute-done.4.refs_2_ = bf16[8,2048]{1,0:T(8,128)(2,1)S(1)} collective-permute-done((bf16[8,2048]{1,0:T(8,128)(2,1)S(1)}, bf16[8,2048]{1,0:T(8,128)(2,1)S(1)}, u32[]{:S(2)}, u32[]{:S(2)}) %collective-permute-start.4) | collective-permute-done | bytes 32800 | tf_op jit(solution)/shard_map/ppermute | solution.py:271
  15.4 0.9 %collective-permute-done.5.refs_3_ = bf16[8,2048]{1,0:T(8,128)(2,1)S(1)} collective-permute-done((bf16[8,2048]{1,0:T(8,128)(2,1)S(1)}, bf16[8,2048]{1,0:T(8,128)(2,1)S(1)}, u32[]{:S(2)}, u32[]{:S(2)}) %collective-permute-start.5) | collective-permute-done | bytes 32800 | tf_op jit(solution)/shard_map/ppermute | solution.py:271
  16.3 2.6 %collective-permute-start.8 = (bf16[8,2048]{1,0:T(8,128)(2,1)S(1)}, bf16[8,2048]{1,0:T(8,128)(2,1)S(1)}, u32[]{:S(2)}, u32[]{:S(2)}) collective-permute-start(bf16[8,2048]{1,0:T(8,128)(2,1)S(1)} %get-tuple-element.26), channel_id=1, source_target_pairs={{0,12},{4,8},{8,4},{12,0},{16,28},{20,24},{24,20},{28,16},{1,13},{... | collective-permute-start | bytes 98312 | tf_op jit(solution)/shard_map/ppermute | solution.py:271
  18.9 0.5 %collective-permute-start.7 = (bf16[8,2048]{1,0:T(8,128)(2,1)S(1)}, bf16[8,2048]{1,0:T(8,128)(2,1)S(1)}, u32[]{:S(2)}, u32[]{:S(2)}) collective-permute-start(bf16[8,2048]{1,0:T(8,128)(2,1)S(1)} %get-tuple-element.26), channel_id=1, source_target_pairs={{0,8},{4,12},{8,0},{12,4},{16,24},{20,28},{24,16},{28,20},{1,9},{5... | collective-permute-start | bytes 98312 | tf_op jit(solution)/shard_map/ppermute | solution.py:271
  19.3 0.5 %collective-permute-start.6 = (bf16[8,2048]{1,0:T(8,128)(2,1)S(1)}, bf16[8,2048]{1,0:T(8,128)(2,1)S(1)}, u32[]{:S(2)}, u32[]{:S(2)}) collective-permute-start(bf16[8,2048]{1,0:T(8,128)(2,1)S(1)} %get-tuple-element.26), channel_id=1, source_target_pairs={{0,4},{4,0},{8,12},{12,8},{16,20},{20,16},{24,28},{28,24},{1,5},{5... | collective-permute-start | bytes 98312 | tf_op jit(solution)/shard_map/ppermute | solution.py:271
  19.8 1.3 %collective-permute-done.8.refs_3_ = bf16[8,2048]{1,0:T(8,128)(2,1)S(1)} collective-permute-done((bf16[8,2048]{1,0:T(8,128)(2,1)S(1)}, bf16[8,2048]{1,0:T(8,128)(2,1)S(1)}, u32[]{:S(2)}, u32[]{:S(2)}) %collective-permute-start.8) | collective-permute-done | bytes 32800 | tf_op jit(solution)/shard_map/ppermute | solution.py:271
  21.1 1.6 %collective-permute-done.7.refs_2_ = bf16[8,2048]{1,0:T(8,128)(2,1)S(1)} collective-permute-done((bf16[8,2048]{1,0:T(8,128)(2,1)S(1)}, bf16[8,2048]{1,0:T(8,128)(2,1)S(1)}, u32[]{:S(2)}, u32[]{:S(2)}) %collective-permute-start.7) | collective-permute-done | bytes 32800 | tf_op jit(solution)/shard_map/ppermute | solution.py:271
  22.8 0.5 %collective-permute-done.6.refs_1_ = bf16[8,2048]{1,0:T(8,128)(2,1)S(1)} collective-permute-done((bf16[8,2048]{1,0:T(8,128)(2,1)S(1)}, bf16[8,2048]{1,0:T(8,128)(2,1)S(1)}, u32[]{:S(2)}, u32[]{:S(2)}) %collective-permute-start.6) | collective-permute-done | bytes 32800 | tf_op jit(solution)/shard_map/ppermute | solution.py:271
  23.2 0.3 time_filter.1
  23.5 2.6 %collective-permute-start.9 = (bf16[8,2048]{1,0:T(8,128)(2,1)S(1)}, bf16[8,2048]{1,0:T(8,128)(2,1)S(1)}, u32[]{:S(2)}, u32[]{:S(2)}) collective-permute-start(bf16[8,2048]{1,0:T(8,128)(2,1)S(1)} %get-tuple-element.28), channel_id=1, source_target_pairs={{0,16},{4,20},{8,24},{12,28},{16,0},{20,4},{24,8},{28,12},{1,17},{... | collective-permute-start | bytes 98312 | tf_op jit(solution)/shard_map/ppermute | solution.py:271
  26.1 2.2 %collective-permute-done.9.refs_1_ = bf16[8,2048]{1,0:T(8,128)(2,1)S(1)} collective-permute-done((bf16[8,2048]{1,0:T(8,128)(2,1)S(1)}, bf16[8,2048]{1,0:T(8,128)(2,1)S(1)}, u32[]{:S(2)}, u32[]{:S(2)}) %collective-permute-start.9) | collective-permute-done | bytes 32800 | tf_op jit(solution)/shard_map/ppermute | solution.py:271
  28.4 0.6 %add_up.1 = f32[8,2048]{1,0:T(8,128)} custom-call(f32[8,2048]{1,0:T(8,128)S(1)} %get-tuple-element.27.refs_0_, bf16[8,2048]{1,0:T(8,128)(2,1)S(1)} %collective-permute-done.9.refs_1_), custom_call_target="tpu_custom_call" | custom-call | tf_op jit(solution)/shard_map/add_up/pallas_call | solution.py:260
  (9 shorter events, 0.0 us)
Async XLA Ops:
  0.0 8.1 %copy-start.1 = (s32[16,8]{0,1:T(8,128)S(1)}, s32[16,8]{0,1:T(8,128)}, u32[]{:S(2)}) copy-start(s32[16,8]{0,1:T(8,128)} %param.7) | copy-start | bytes 1540
  0.9 7.3 %collective-permute-start.2 = (bf16[8,2048]{1,0:T(8,128)(2,1)S(1)}, bf16[8,2048]{1,0:T(8,128)(2,1)S(1)}, u32[]{:S(2)}, u32[]{:S(2)}) collective-permute-start(bf16[8,2048]{1,0:T(8,128)(2,1)S(1)} %convert_element_type.3.refs_0_), channel_id=1, source_target_pairs={{0,3},{1,2},{2,1},{3,0},{4,7},{5,6},{6,5},{7,4},{8,11},{9,10},{10,... | collective-permute-start | bytes 98312 | tf_op jit(solution)/shard_map/ppermute | solution.py:271
  3.2 4.9 %collective-permute-start.1 = (bf16[8,2048]{1,0:T(8,128)(2,1)S(1)}, bf16[8,2048]{1,0:T(8,128)(2,1)S(1)}, u32[]{:S(2)}, u32[]{:S(2)}) collective-permute-start(bf16[8,2048]{1,0:T(8,128)(2,1)S(1)} %convert_element_type.3.refs_0_), channel_id=1, source_target_pairs={{0,2},{1,3},{2,0},{3,1},{4,6},{5,7},{6,4},{7,5},{8,10},{9,11},{10,... | collective-permute-start | bytes 98312 | tf_op jit(solution)/shard_map/ppermute | solution.py:271
  3.8 4.3 %collective-permute-start = (bf16[8,2048]{1,0:T(8,128)(2,1)S(1)}, bf16[8,2048]{1,0:T(8,128)(2,1)S(1)}, u32[]{:S(2)}, u32[]{:S(2)}) collective-permute-start(bf16[8,2048]{1,0:T(8,128)(2,1)S(1)} %convert_element_type.3.refs_0_), channel_id=1, source_target_pairs={{0,1},{1,0},{2,3},{3,2},{4,5},{5,4},{6,7},{7,6},{8,9},{9,8},{10,11... | collective-permute-start | bytes 98312 | tf_op jit(solution)/shard_map/ppermute | solution.py:271
  4.0 0.7 %copy-start = (f32[1023]{0:T(1024)S(1)}, f32[1023]{0:T(1024)}, u32[]{:S(2)}) copy-start(f32[1023]{0:T(1024)} %param.9) | copy-start | bytes 12280
  4.7 0.7 %copy-start.2 = (s32[1,8]{1,0:T(1,128)S(1)}, s32[1,8]{1,0:T(1,128)}, u32[]{:S(2)}) copy-start(s32[1,8]{1,0:T(1,128)} %sizes_hbm.1) | copy-start | bytes 100
  11.0 2.0 %collective-permute-start.3 = (bf16[8,2048]{1,0:T(8,128)(2,1)S(1)}, bf16[8,2048]{1,0:T(8,128)(2,1)S(1)}, u32[]{:S(2)}, u32[]{:S(2)}) collective-permute-start(bf16[8,2048]{1,0:T(8,128)(2,1)S(1)} %get-tuple-element.22), channel_id=1, source_target_pairs={{0,1},{1,0},{2,3},{3,2},{4,5},{5,4},{6,7},{7,6},{8,9},{9,8},{10,11... | collective-permute-start | bytes 98312 | tf_op jit(solution)/shard_map/ppermute | solution.py:271
  11.4 3.9 %collective-permute-start.4 = (bf16[8,2048]{1,0:T(8,128)(2,1)S(1)}, bf16[8,2048]{1,0:T(8,128)(2,1)S(1)}, u32[]{:S(2)}, u32[]{:S(2)}) collective-permute-start(bf16[8,2048]{1,0:T(8,128)(2,1)S(1)} %get-tuple-element.23), channel_id=1, source_target_pairs={{0,2},{1,3},{2,0},{3,1},{4,6},{5,7},{6,4},{7,5},{8,10},{9,11},{10,... | collective-permute-start | bytes 98312 | tf_op jit(solution)/shard_map/ppermute | solution.py:271
  12.9 3.4 %collective-permute-start.5 = (bf16[8,2048]{1,0:T(8,128)(2,1)S(1)}, bf16[8,2048]{1,0:T(8,128)(2,1)S(1)}, u32[]{:S(2)}, u32[]{:S(2)}) collective-permute-start(bf16[8,2048]{1,0:T(8,128)(2,1)S(1)} %get-tuple-element.24), channel_id=1, source_target_pairs={{0,3},{1,2},{2,1},{3,0},{4,7},{5,6},{6,5},{7,4},{8,11},{9,10},{10,... | collective-permute-start | bytes 98312 | tf_op jit(solution)/shard_map/ppermute | solution.py:271
  16.3 4.9 %collective-permute-start.8 = (bf16[8,2048]{1,0:T(8,128)(2,1)S(1)}, bf16[8,2048]{1,0:T(8,128)(2,1)S(1)}, u32[]{:S(2)}, u32[]{:S(2)}) collective-permute-start(bf16[8,2048]{1,0:T(8,128)(2,1)S(1)} %get-tuple-element.26), channel_id=1, source_target_pairs={{0,12},{4,8},{8,4},{12,0},{16,28},{20,24},{24,20},{28,16},{1,13},{... | collective-permute-start | bytes 98312 | tf_op jit(solution)/shard_map/ppermute | solution.py:271
  18.9 3.9 %collective-permute-start.7 = (bf16[8,2048]{1,0:T(8,128)(2,1)S(1)}, bf16[8,2048]{1,0:T(8,128)(2,1)S(1)}, u32[]{:S(2)}, u32[]{:S(2)}) collective-permute-start(bf16[8,2048]{1,0:T(8,128)(2,1)S(1)} %get-tuple-element.26), channel_id=1, source_target_pairs={{0,8},{4,12},{8,0},{12,4},{16,24},{20,28},{24,16},{28,20},{1,9},{5... | collective-permute-start | bytes 98312 | tf_op jit(solution)/shard_map/ppermute | solution.py:271
  19.3 3.9 %collective-permute-start.6 = (bf16[8,2048]{1,0:T(8,128)(2,1)S(1)}, bf16[8,2048]{1,0:T(8,128)(2,1)S(1)}, u32[]{:S(2)}, u32[]{:S(2)}) collective-permute-start(bf16[8,2048]{1,0:T(8,128)(2,1)S(1)} %get-tuple-element.26), channel_id=1, source_target_pairs={{0,4},{4,0},{8,12},{12,8},{16,20},{20,16},{24,28},{28,24},{1,5},{5... | collective-permute-start | bytes 98312 | tf_op jit(solution)/shard_map/ppermute | solution.py:271
  23.5 4.9 %collective-permute-start.9 = (bf16[8,2048]{1,0:T(8,128)(2,1)S(1)}, bf16[8,2048]{1,0:T(8,128)(2,1)S(1)}, u32[]{:S(2)}, u32[]{:S(2)}) collective-permute-start(bf16[8,2048]{1,0:T(8,128)(2,1)S(1)} %get-tuple-element.28), channel_id=1, source_target_pairs={{0,16},{4,20},{8,24},{12,28},{16,0},{20,4},{24,8},{28,12},{1,17},{... | collective-permute-start | bytes 98312 | tf_op jit(solution)/shard_map/ppermute | solution.py:271

commit v2 on v1

v2 whole, which is shorter than its diff:
```python
import functools
import jax
import jax.numpy as jnp
from jax import lax
from jax.experimental import pallas as pl
from jax.experimental.pallas import tpu as pltpu
from jax.sharding import PartitionSpec as P

VMEM = pl.BlockSpec(memory_space=pltpu.VMEM)
HBM = pl.BlockSpec(memory_space=pltpu.HBM)
NT = (((1,), (1,)), ((), ()))
LIMIT = 16 * 2**20
DIRECT = 8
NEAR = 4


def three_parts(value):
    high = value.astype(jnp.bfloat16)
    rest = value - high.astype(jnp.float32)
    middle = rest.astype(jnp.bfloat16)
    low = (rest - middle.astype(jnp.float32)).astype(jnp.bfloat16)
    return high, middle, low


def ahead(snapshots, half_width, width):
    return -(-max(0, snapshots + width - half_width) // 128) * 128


def hold_kernel(weights_ref, held_ref, turned_ref, sems):
    zone_blocks, slots, _, _ = weights_ref.shape
    parts = sems.shape[0]
    each = zone_blocks // parts
    copies = [
        pltpu.make_async_copy(
            weights_ref.at[pl.ds(n * each, each)], held_ref.at[pl.ds(n * each, each)], sems.at[n]
        )
        for n in range(parts)
    ]
    for copy in copies:
        copy.start()
    for n, copy in enumerate(copies):
        copy.wait()
        for i in range(n * each, min((n + 1) * each, turned_ref.shape[0])):
            for k in range(slots):
                turned_ref[i, k] = held_ref[i, k].T


def hold(weights):
    zone_blocks = weights.shape[0]
    turned = zone_blocks - zone_blocks // 4
    return pl.pallas_call(
        hold_kernel,
        out_shape=[
            jax.ShapeDtypeStruct((count, *weights.shape[1:]), weights.dtype)
            for count in (zone_blocks, turned)
        ],
        in_specs=[HBM],
        out_specs=[VMEM] * 2,
        scratch_shapes=[pltpu.SemaphoreType.DMA((min(4, weights.shape[0]),))],
        compiler_params=pltpu.CompilerParams(vmem_limit_bytes=43 * 2**20),
        cost_estimate=pl.CostEstimate(flops=0, bytes_accessed=8 * 2**20, transcendentals=0),
        name="hold",
    )(weights)


def prepare_kernel(where_ref, taps_ref, rows_ref, line_ref):
    taps_total = taps_ref.shape[1]
    rows, width = line_ref.shape
    half_width = (taps_total - 1) // 2
    steps = rows_ref.shape[0] // rows
    before = ahead(steps * rows_ref.shape[1], half_width, rows_ref.shape[1])
    line_ref[...] = jnp.zeros_like(line_ref)
    line_ref[:, before : before + taps_total] = jnp.broadcast_to(
        taps_ref[...], (rows, taps_total)
    )
    line = line_ref[...]
    row_ids = lax.broadcasted_iota(jnp.int32, (rows, 1), 0)
    slanted = line
    for r in range(1, rows):
        slanted = jnp.where(row_ids == r, pltpu.roll(line, r, 1), slanted)
    line_ref[...] = slanted
    near = rows_ref.shape[1] // rows
    lanes = lax.broadcasted_iota(jnp.int32, (rows, near * rows), 1)
    at = where_ref[0, 1]
    for step in range(steps):
        target = at ^ (near * step) if steps <= DIRECT else near * step + (at & (near - 1))
        found = jnp.zeros((rows, near * rows), jnp.float32)
        for n in range(near):
            base = ((at ^ n) - target) * rows + half_width - n * rows + before
            first = pl.multiple_of((base >> 7) << 7, 128)
            window = line_ref[:, pl.ds(first, 256)]
            turned = pltpu.roll(window, (256 - (base & 127)) & 255, 1)
            found = jnp.where(lanes >= n * rows, turned[:, : near * rows], found)
        rows_ref[step * rows : (step + 1) * rows, :] = found


def prepare(where, filter_taps, steps, near, rows):
    taps_total = filter_taps.shape[0]
    half_width = (taps_total - 1) // 2
    snapshots = near * steps * rows
    width = ahead(snapshots, half_width, near * rows) + max(taps_total + rows, half_width + snapshots) + 256
    width = -(-width // 128) * 128
    return pl.pallas_call(
        prepare_kernel,
        out_shape=jax.ShapeDtypeStruct((steps * rows, near * rows), jnp.float32),
        in_specs=[VMEM] * 2,
        out_specs=VMEM,
        scratch_shapes=[pltpu.VMEM((rows, width), jnp.float32)],
        compiler_params=pltpu.CompilerParams(vmem_limit_bytes=LIMIT),
        cost_estimate=pl.CostEstimate(flops=0, bytes_accessed=4 * 2**20, transcendentals=0),
        name="prepare",
    )(where, filter_taps.reshape(1, -1))


def remap_kernel(zones, where_ref, columns_ref, sizes_ref, *refs):
    x_refs, (weights_ref, turned_ref, *refs) = refs[:zones], refs[zones:]
    c_refs, (blocks_ref, total_ref) = refs[:zones], refs[zones:]
    zone_blocks, slots, size, _ = weights_ref.shape
    rows = x_refs[0].shape[0]
    me = where_ref[0, 0]
    for step in range(zones):
        first = (me ^ (zones - step if step else 0)) * zone_blocks
        for b in range(zone_blocks):
            blocks_ref[first + b] = x_refs[step][:, b * size : (b + 1) * size].astype(jnp.float32)
    total_ref[...] = jnp.zeros_like(total_ref)

    pieces = []
    for i in range(zone_blocks):
        picked = jnp.concatenate([blocks_ref[columns_ref[k, i]] for k in range(slots)], axis=1)
        picked = picked.astype(jnp.bfloat16)
        if i < turned_ref.shape[0]:
            block = turned_ref[i].reshape(slots * size, size)
            wind = jnp.dot(picked, block, preferred_element_type=jnp.float32)
        else:
            wide = jnp.concatenate([weights_ref[i, k] for k in range(slots)], axis=1)
            wind = lax.dot_general(picked, wide, NT, preferred_element_type=jnp.float32)
        pieces.append(wind * jnp.abs(wind))
    stress = jnp.concatenate(pieces, axis=1)

    basins, cells = sizes_ref.shape[1], x_refs[0].shape[1]
    cell_ids = lax.broadcasted_iota(jnp.int32, (1, cells), 1)
    basin_ids = jnp.zeros((1, cells), jnp.int32)
    basin_lanes = lax.broadcasted_iota(jnp.int32, (1, basins), 1)
    counts = jnp.zeros((1, basins), jnp.int32)
    end = 0
    for g in range(basins):
        counts = jnp.where(basin_lanes == g, sizes_ref[0, g], counts)
        if g:
            basin_ids += (cell_ids >= end).astype(jnp.int32)
        end = end + sizes_ref[0, g]
    member = lax.broadcasted_iota(jnp.int32, (basins, cells), 0) == basin_ids
    member = member.astype(jnp.float32).astype(jnp.bfloat16)
    parts = lax.dot_general(
        jnp.concatenate(three_parts(stress), axis=0), member, NT, preferred_element_type=jnp.float32
    )
    totals = parts[:rows] + parts[rows : 2 * rows] + parts[2 * rows :]
    means = totals / counts.astype(jnp.float32)
    spread = jnp.dot(
        jnp.concatenate(three_parts(means), axis=0), member, preferred_element_type=jnp.float32
    )
    anomaly = stress - (spread[:rows] + spread[rows : 2 * rows] + spread[2 * rows :])

    high = anomaly.astype(jnp.bfloat16)
    low = (anomaly - high.astype(jnp.float32)).astype(jnp.bfloat16)
    both = jnp.concatenate([high, low], axis=0)
    for i in range(zone_blocks):
        wide = jnp.concatenate([weights_ref[i, k] for k in range(slots)], axis=1)
        back = jnp.dot(
            both[:, i * size : (i + 1) * size], wide, preferred_element_type=jnp.float32
        )
        back = back[:rows] + back[rows:]
        targets = [columns_ref[k, i] for k in range(slots)]
        before = [total_ref[column] for column in targets]
        for k in range(slots):
            total_ref[targets[k]] = before[k] + back[:, k * size : (k + 1) * size]
    for step in range(zones):
        first = (me ^ step) * zone_blocks
        for b in range(zone_blocks):
            c_refs[step][:, b * size : (b + 1) * size] = total_ref[first + b].astype(
                c_refs[step].dtype
            )


def remap(where, columns, sizes, xs, weights, turned):
    zones = len(xs)
    rows, cells = xs[0].shape
    all_blocks = zones * weights.shape[0]
    size = weights.shape[2]
    outs = [
        jax.ShapeDtypeStruct((rows, cells), jnp.bfloat16 if step else jnp.float32)
        for step in range(zones)
    ]
    return pl.pallas_call(
        functools.partial(remap_kernel, zones),
        out_shape=outs,
        in_specs=[VMEM] * (5 + zones),
        out_specs=[VMEM] * zones,
        scratch_shapes=[
            pltpu.VMEM((all_blocks, rows, size), jnp.float32),
            pltpu.VMEM((all_blocks, rows, size), jnp.float32),
        ],
        compiler_params=pltpu.CompilerParams(vmem_limit_bytes=LIMIT),
        cost_estimate=pl.CostEstimate(flops=10**8, bytes_accessed=8 * 2**20, transcendentals=0),
        name="remap",
    )(where, columns, sizes, *xs, weights, turned)


def gather_kernel(taps_ref, *refs):
    *parts, total_ref, low_ref = refs
    del taps_ref
    total = sum(r[...].astype(jnp.float32) for r in parts)
    total_ref[...] = total
    low_ref[...] = total.astype(low_ref.dtype)


def add_zones(taps, parts):
    return pl.pallas_call(
        gather_kernel,
        out_shape=[jax.ShapeDtypeStruct(parts[0].shape, d) for d in (jnp.float32, jnp.bfloat16)],
        in_specs=[VMEM] * (1 + len(parts)),
        out_specs=[VMEM] * 2,
        compiler_params=pltpu.CompilerParams(vmem_limit_bytes=LIMIT),
        name="add_zones",
    )(taps, *parts)


def filter_kernel(near, taps_ref, *refs):
    values, outs = refs[:near], refs[near:]
    rows = values[0].shape[0]
    values = [values[0], *values[:0:-1]]
    together = jnp.concatenate([r[...].astype(jnp.float32) for r in values], axis=0)
    result = jnp.dot(
        taps_ref[...], together, precision=lax.Precision.HIGHEST, preferred_element_type=jnp.float32
    )
    if len(outs) == 1:
        outs[0][...] = result.astype(outs[0].dtype)
        return
    for step, out in enumerate(outs):
        out[...] = result[step * rows : (step + 1) * rows].astype(out.dtype)


def time_filter(taps, values):
    rows, cells = values[0].shape
    steps = taps.shape[0] // rows
    if steps <= DIRECT:
        outs = [
            jax.ShapeDtypeStruct((rows, cells), jnp.bfloat16 if step else jnp.float32)
            for step in range(steps)
        ]
    else:
        outs = [jax.ShapeDtypeStruct((steps * rows, cells), jnp.bfloat16)]
    return pl.pallas_call(
        functools.partial(filter_kernel, len(values)),
        out_shape=outs,
        in_specs=[VMEM] * (1 + len(values)),
        out_specs=[VMEM] * len(outs),
        compiler_params=pltpu.CompilerParams(vmem_limit_bytes=LIMIT),
        name="time_filter",
    )(taps, *values)


def sum_kernel(*refs):
    refs[-1][...] = sum(r[...].astype(jnp.float32) for r in refs[:-1])


def add_up(parts):
    return pl.pallas_call(
        sum_kernel,
        out_shape=jax.ShapeDtypeStruct(parts[0].shape, jnp.float32),
        in_specs=[VMEM] * len(parts),
        out_specs=VMEM,
        compiler_params=pltpu.CompilerParams(vmem_limit_bytes=LIMIT),
        name="add_up",
    )(*parts)


def swap(value, axis, by):
    return lax.ppermute(value, axis, [(i, i ^ by) for i in range(lax.axis_size(axis))])


def shards(source_field, remap_weights, block_columns, piece_sizes, filter_taps):
    rows, cells = source_field.shape
    zones, owners = lax.axis_size("zone"), lax.axis_size("tm")
    near = min(NEAR, owners)
    steps = owners // near
    where = jnp.stack([lax.axis_index("zone"), lax.axis_index("tm")]).reshape(1, 2)
    xlow = source_field.astype(jnp.bfloat16)
    xs = [xlow] + [swap(xlow, "zone", step) for step in range(zones - 1, 0, -1)]
    held, turned = hold(remap_weights)
    sent = remap(where, block_columns.T, piece_sizes, xs, held, turned)
    taps = prepare(where, filter_taps, steps, near, rows)
    summed, low = add_zones(
        taps, [sent[0]] + [swap(sent[step], "zone", step) for step in range(zones - 1, 0, -1)]
    )
    others = [swap(low, "tm", n) for n in range(near - 1, 0, -1)]
    parts = time_filter(taps, [summed] + others)
    if steps <= DIRECT:
        last = [parts[0]] + [swap(parts[step], "tm", near * step) for step in range(1, steps)]
        return add_up(last)
    groups = [list(range(side, owners, near)) for side in range(near)]
    parts = lax.all_to_all(
        parts[0].reshape(steps, rows, cells), "tm", 0, 0, axis_index_groups=groups
    )
    return parts.astype(jnp.float32).sum(axis=0)


def solution(mesh):
    return jax.shard_map(
        shards,
        mesh=mesh,
        in_specs=(
            P("tm", "zone"),
            P("zone", None, None, None),
            P("zone", None),
            P("zone", None),
            P(),
        ),
        out_specs=P("tm", "zone"),
        check_vma=False,
    )
```

time: 29.3 us -> 26.7 us (0.911)
  local copies, waits for them, and re-layouts: 1.34 us -> 0.01 us
  Pallas kernels: 6.5 us -> 5.23 us
    unnamed x6, local copies, waits for them, and re-layouts: 1.34 us -> 0.01 us
    pallas_call x1, Pallas kernels: 2.79 us -> 1.83 us  [remap(): pl.pallas_call(functools.partial(remap_kernel, zones), out_shape=outs, in...]
    pallas_call x1 -> x2, Pallas kernels: 2.77 us -> 2.46 us  [the longest x1 2.23 us: hold(): pl.pallas_call(hold_kernel, out_shape=[jax.ShapeDtypeStruct((count, *weig...]
  transfers between devices with their start and end apart: 10 -> 10, of which waited for: 6 -> 7; matrix products, arithmetic and copies ran while one was open for 0% -> 0% of each run, Pallas kernels for 10% -> 9%
where the time goes in v2:
time: 26.7 us; the launch traced here: 26.5 us
  starting transfers between devices  11.2 us (42%)
  waiting for transfers between devices  9.09 us (34%)
  Pallas kernels  5.23 us (20%)
  other arithmetic  0.95 us (4%)
    ppermute x10, starting transfers between devices, swap(): lax.ppermute(value, axis, [(i, i ^ by) for i in range(lax.axis_size(axis))])  11.2 us
    ppermute x10, waiting for transfers between devices, swap(): lax.ppermute(value, axis, [(i, i ^ by) for i in range(lax.axis_size(axis))])  9.09 us
    pallas_call x1, Pallas kernels, hold(): pl.pallas_call(hold_kernel, out_shape=[jax.ShapeDtypeStruct((count, *weig...  2.23 us
    pallas_call x1, Pallas kernels, remap(): pl.pallas_call(functools.partial(remap_kernel, zones), out_shape=outs, in...  1.83 us
    convert_element_type x1, other arithmetic, shards(): xlow = source_field.astype(jnp.bfloat16)  0.87 us
    pallas_call x1, Pallas kernels, add_up(): pl.pallas_call(sum_kernel, out_shape=jax.ShapeDtypeStruct(parts[0].shape,...  0.64 us
  transfers between devices with their start and end apart: 10, of which 7 were waited for; matrix products, arithmetic and copies ran while one was open for 0% of the time, Pallas kernels for 9%

profile of v2, /device:TPU:0, one launch (start us, length us, event | category | flops | bytes accessed | tf_op | source)
XLA Modules:
  0.0 26.5 jit_solution(6747313251352909831)
XLA Ops:
  0.0 0.9 %convert_element_type.3.refs_0_ = bf16[8,2048]{1,0:T(8,128)(2,1)S(1)} convert(f32[8,2048]{1,0:T(8,128)} %param.5) | non-fusion elementwise | flops 16384 | bytes 98304 | tf_op jit(solution)/shard_map/convert_element_type | solution.py:287
  0.9 2.4 %collective-permute-start = (bf16[8,2048]{1,0:T(8,128)(2,1)S(1)}, bf16[8,2048]{1,0:T(8,128)(2,1)S(1)}, u32[]{:S(2)}, u32[]{:S(2)}) collective-permute-start(bf16[8,2048]{1,0:T(8,128)(2,1)S(1)} %convert_element_type.3.refs_0_), channel_id=1, source_target_pairs={{0,3},{1,2},{2,1},{3,0},{4,7},{5,6},{6,5},{7,4},{8,11},{9,10},{10,... | collective-permute-start | bytes 98312 | tf_op jit(solution)/shard_map/ppermute | solution.py:278
  3.3 0.6 %collective-permute-start.1 = (bf16[8,2048]{1,0:T(8,128)(2,1)S(1)}, bf16[8,2048]{1,0:T(8,128)(2,1)S(1)}, u32[]{:S(2)}, u32[]{:S(2)}) collective-permute-start(bf16[8,2048]{1,0:T(8,128)(2,1)S(1)} %convert_element_type.3.refs_0_), channel_id=1, source_target_pairs={{0,2},{1,3},{2,0},{3,1},{4,6},{5,7},{6,4},{7,5},{8,10},{9,11},{10,... | collective-permute-start | bytes 98312 | tf_op jit(solution)/shard_map/ppermute | solution.py:278
  3.8 0.1 collective-permute-start.2
  3.9 0.1 add_bitcast_fusion.where_ref
  4.0 2.2 %hold.1 = (bf16[16,8,128,128]{3,2,1,0:T(8,128)(2,1)S(1)}, bf16[12,8,128,128]{3,2,1,0:T(8,128)(2,1)S(1)}) custom-call(bf16[16,8,128,128]{3,2,1,0:T(8,128)(2,1)} %weights_ref.1), custom_call_target="tpu_custom_call" | custom-call | bytes 8388608 | tf_op jit(solution)/shard_map/hold/pallas_call | solution.py:51
  6.3 1.0 %collective-permute-done.1.refs_2_ = bf16[8,2048]{1,0:T(8,128)(2,1)S(1)} collective-permute-done((bf16[8,2048]{1,0:T(8,128)(2,1)S(1)}, bf16[8,2048]{1,0:T(8,128)(2,1)S(1)}, u32[]{:S(2)}, u32[]{:S(2)}) %collective-permute-start.1) | collective-permute-done | bytes 32800 | tf_op jit(solution)/shard_map/ppermute | solution.py:278
  7.2 1.8 %remap.1 = (f32[8,2048]{1,0:T(8,128)S(1)}, bf16[8,2048]{1,0:T(8,128)(2,1)S(1)}, bf16[8,2048]{1,0:T(8,128)(2,1)S(1)}, bf16[8,2048]{1,0:T(8,128)(2,1)S(1)}) custom-call(s32[1,2]{1,0:T(1,128)S(1)} %add_bitcast_fusion.where_ref, s32[8,16]{1,0:T(8,128)S(1)} %bitcast.6, s32[1,8]{1,0:T(1,128)S(1)} %copy-done.2, bf16[8,2048]{1,0:T(8,128)(2,1)S(1)} %convert_element_type.3.refs_0_, ...), custom_call_target="tpu_custom_call" | custom-call | flops 100000000 | bytes 8388608 | tf_op jit(solution)/shard_map/remap/pallas_call | solution.py:193
  9.1 0.8 %collective-permute-start.3 = (bf16[8,2048]{1,0:T(8,128)(2,1)S(1)}, bf16[8,2048]{1,0:T(8,128)(2,1)S(1)}, u32[]{:S(2)}, u32[]{:S(2)}) collective-permute-start(bf16[8,2048]{1,0:T(8,128)(2,1)S(1)} %get-tuple-element.18), channel_id=1, source_target_pairs={{0,3},{1,2},{2,1},{3,0},{4,7},{5,6},{6,5},{7,4},{8,11},{9,10},{10,... | collective-permute-start | bytes 98312 | tf_op jit(solution)/shard_map/ppermute | solution.py:278
  9.8 0.8 %collective-permute-start.4 = (bf16[8,2048]{1,0:T(8,128)(2,1)S(1)}, bf16[8,2048]{1,0:T(8,128)(2,1)S(1)}, u32[]{:S(2)}, u32[]{:S(2)}) collective-permute-start(bf16[8,2048]{1,0:T(8,128)(2,1)S(1)} %get-tuple-element.19), channel_id=1, source_target_pairs={{0,2},{1,3},{2,0},{3,1},{4,6},{5,7},{6,4},{7,5},{8,10},{9,11},{10,... | collective-permute-start | bytes 98312 | tf_op jit(solution)/shard_map/ppermute | solution.py:278
  10.6 0.4 %collective-permute-start.5 = (bf16[8,2048]{1,0:T(8,128)(2,1)S(1)}, bf16[8,2048]{1,0:T(8,128)(2,1)S(1)}, u32[]{:S(2)}, u32[]{:S(2)}) collective-permute-start(bf16[8,2048]{1,0:T(8,128)(2,1)S(1)} %get-tuple-element.20), channel_id=1, source_target_pairs={{0,1},{1,0},{2,3},{3,2},{4,5},{5,4},{6,7},{7,6},{8,9},{9,8},{10,11... | collective-permute-start | bytes 98312 | tf_op jit(solution)/shard_map/ppermute | solution.py:278
  11.0 0.2 prepare.1.taps_ref
  11.2 1.6 %collective-permute-done.3.refs_1_ = bf16[8,2048]{1,0:T(8,128)(2,1)S(1)} collective-permute-done((bf16[8,2048]{1,0:T(8,128)(2,1)S(1)}, bf16[8,2048]{1,0:T(8,128)(2,1)S(1)}, u32[]{:S(2)}, u32[]{:S(2)}) %collective-permute-start.3) | collective-permute-done | bytes 32800 | tf_op jit(solution)/shard_map/ppermute | solution.py:278
  12.8 0.9 %collective-permute-done.4.refs_2_ = bf16[8,2048]{1,0:T(8,128)(2,1)S(1)} collective-permute-done((bf16[8,2048]{1,0:T(8,128)(2,1)S(1)}, bf16[8,2048]{1,0:T(8,128)(2,1)S(1)}, u32[]{:S(2)}, u32[]{:S(2)}) %collective-permute-start.4) | collective-permute-done | bytes 32800 | tf_op jit(solution)/shard_map/ppermute | solution.py:278
  13.8 2.6 %collective-permute-start.6 = (bf16[8,2048]{1,0:T(8,128)(2,1)S(1)}, bf16[8,2048]{1,0:T(8,128)(2,1)S(1)}, u32[]{:S(2)}, u32[]{:S(2)}) collective-permute-start(bf16[8,2048]{1,0:T(8,128)(2,1)S(1)} %get-tuple-element.22), channel_id=1, source_target_pairs={{0,12},{4,8},{8,4},{12,0},{16,28},{20,24},{24,20},{28,16},{1,13},{... | collective-permute-start | bytes 98312 | tf_op jit(solution)/shard_map/ppermute | solution.py:278
  16.4 0.4 %collective-permute-start.7 = (bf16[8,2048]{1,0:T(8,128)(2,1)S(1)}, bf16[8,2048]{1,0:T(8,128)(2,1)S(1)}, u32[]{:S(2)}, u32[]{:S(2)}) collective-permute-start(bf16[8,2048]{1,0:T(8,128)(2,1)S(1)} %get-tuple-element.22), channel_id=1, source_target_pairs={{0,8},{4,12},{8,0},{12,4},{16,24},{20,28},{24,16},{28,20},{1,9},{5... | collective-permute-start | bytes 98312 | tf_op jit(solution)/shard_map/ppermute | solution.py:278
  16.8 0.5 %collective-permute-start.8 = (bf16[8,2048]{1,0:T(8,128)(2,1)S(1)}, bf16[8,2048]{1,0:T(8,128)(2,1)S(1)}, u32[]{:S(2)}, u32[]{:S(2)}) collective-permute-start(bf16[8,2048]{1,0:T(8,128)(2,1)S(1)} %get-tuple-element.22), channel_id=1, source_target_pairs={{0,4},{4,0},{8,12},{12,8},{16,20},{20,16},{24,28},{28,24},{1,5},{5... | collective-permute-start | bytes 98312 | tf_op jit(solution)/shard_map/ppermute | solution.py:278
  17.3 1.4 %collective-permute-done.6.refs_1_ = bf16[8,2048]{1,0:T(8,128)(2,1)S(1)} collective-permute-done((bf16[8,2048]{1,0:T(8,128)(2,1)S(1)}, bf16[8,2048]{1,0:T(8,128)(2,1)S(1)}, u32[]{:S(2)}, u32[]{:S(2)}) %collective-permute-start.6) | collective-permute-done | bytes 32800 | tf_op jit(solution)/shard_map/ppermute | solution.py:278
  18.8 1.5 %collective-permute-done.7.refs_2_ = bf16[8,2048]{1,0:T(8,128)(2,1)S(1)} collective-permute-done((bf16[8,2048]{1,0:T(8,128)(2,1)S(1)}, bf16[8,2048]{1,0:T(8,128)(2,1)S(1)}, u32[]{:S(2)}, u32[]{:S(2)}) %collective-permute-start.7) | collective-permute-done | bytes 32800 | tf_op jit(solution)/shard_map/ppermute | solution.py:278
  20.3 0.4 %collective-permute-done.8.refs_3_ = bf16[8,2048]{1,0:T(8,128)(2,1)S(1)} collective-permute-done((bf16[8,2048]{1,0:T(8,128)(2,1)S(1)}, bf16[8,2048]{1,0:T(8,128)(2,1)S(1)}, u32[]{:S(2)}, u32[]{:S(2)}) %collective-permute-start.8) | collective-permute-done | bytes 32800 | tf_op jit(solution)/shard_map/ppermute | solution.py:278
  20.7 0.3 %time_filter.1 = (f32[8,2048]{1,0:T(8,128)S(1)}, bf16[8,2048]{1,0:T(8,128)(2,1)S(1)}) custom-call(f32[16,32]{1,0:T(8,128)S(1)} %prepare.1.taps_ref, f32[8,2048]{1,0:T(8,128)S(1)} %get-tuple-element.21.refs_0_, bf16[8,2048]{1,0:T(8,128)(2,1)S(1)} %collective-permute-done.6.refs_1_, bf16[8,2048]{1,0:T(8,128)(2,1)S(1)} %collective-permute-done.7.refs_2_, ...), custom_call_target="tpu_custom_call" | custom-call | tf_op jit(solution)/shard_map/time_filter/pallas_call | solution.py:252
  21.0 2.6 %collective-permute-start.9 = (bf16[8,2048]{1,0:T(8,128)(2,1)S(1)}, bf16[8,2048]{1,0:T(8,128)(2,1)S(1)}, u32[]{:S(2)}, u32[]{:S(2)}) collective-permute-start(bf16[8,2048]{1,0:T(8,128)(2,1)S(1)} %get-tuple-element.24), channel_id=1, source_target_pairs={{0,16},{4,20},{8,24},{12,28},{16,0},{20,4},{24,8},{28,12},{1,17},{... | collective-permute-start | bytes 98312 | tf_op jit(solution)/shard_map/ppermute | solution.py:278
  23.6 2.2 %collective-permute-done.9.refs_1_ = bf16[8,2048]{1,0:T(8,128)(2,1)S(1)} collective-permute-done((bf16[8,2048]{1,0:T(8,128)(2,1)S(1)}, bf16[8,2048]{1,0:T(8,128)(2,1)S(1)}, u32[]{:S(2)}, u32[]{:S(2)}) %collective-permute-start.9) | collective-permute-done | bytes 32800 | tf_op jit(solution)/shard_map/ppermute | solution.py:278
  25.9 0.6 %add_up.1 = f32[8,2048]{1,0:T(8,128)} custom-call(f32[8,2048]{1,0:T(8,128)S(1)} %get-tuple-element.23.refs_0_, bf16[8,2048]{1,0:T(8,128)(2,1)S(1)} %collective-permute-done.9.refs_1_), custom_call_target="tpu_custom_call" | custom-call | tf_op jit(solution)/shard_map/add_up/pallas_call | solution.py:267
  (10 shorter events, 0.0 us)
Async XLA Ops:
  0.0 7.2 %copy-start = (s32[16,8]{0,1:T(8,128)S(1)}, s32[16,8]{0,1:T(8,128)}, u32[]{:S(2)}) copy-start(s32[16,8]{0,1:T(8,128)} %param.7) | copy-start | bytes 1540
  0.0 7.2 %copy-start.2 = (s32[1,8]{1,0:T(1,128)S(1)}, s32[1,8]{1,0:T(1,128)}, u32[]{:S(2)}) copy-start(s32[1,8]{1,0:T(1,128)} %sizes_ref.1) | copy-start | bytes 100
  0.9 5.4 %collective-permute-start = (bf16[8,2048]{1,0:T(8,128)(2,1)S(1)}, bf16[8,2048]{1,0:T(8,128)(2,1)S(1)}, u32[]{:S(2)}, u32[]{:S(2)}) collective-permute-start(bf16[8,2048]{1,0:T(8,128)(2,1)S(1)} %convert_element_type.3.refs_0_), channel_id=1, source_target_pairs={{0,3},{1,2},{2,1},{3,0},{4,7},{5,6},{6,5},{7,4},{8,11},{9,10},{10,... | collective-permute-start | bytes 98312 | tf_op jit(solution)/shard_map/ppermute | solution.py:278
  3.3 4.0 %collective-permute-start.1 = (bf16[8,2048]{1,0:T(8,128)(2,1)S(1)}, bf16[8,2048]{1,0:T(8,128)(2,1)S(1)}, u32[]{:S(2)}, u32[]{:S(2)}) collective-permute-start(bf16[8,2048]{1,0:T(8,128)(2,1)S(1)} %convert_element_type.3.refs_0_), channel_id=1, source_target_pairs={{0,2},{1,3},{2,0},{3,1},{4,6},{5,7},{6,4},{7,5},{8,10},{9,11},{10,... | collective-permute-start | bytes 98312 | tf_op jit(solution)/shard_map/ppermute | solution.py:278
  3.8 3.4 %collective-permute-start.2 = (bf16[8,2048]{1,0:T(8,128)(2,1)S(1)}, bf16[8,2048]{1,0:T(8,128)(2,1)S(1)}, u32[]{:S(2)}, u32[]{:S(2)}) collective-permute-start(bf16[8,2048]{1,0:T(8,128)(2,1)S(1)} %convert_element_type.3.refs_0_), channel_id=1, source_target_pairs={{0,1},{1,0},{2,3},{3,2},{4,5},{5,4},{6,7},{7,6},{8,9},{9,8},{10,11... | collective-permute-start | bytes 98312 | tf_op jit(solution)/shard_map/ppermute | solution.py:278
  6.3 4.8 %copy-start.1 = (f32[1023]{0:T(1024)S(1)}, f32[1023]{0:T(1024)}, u32[]{:S(2)}) copy-start(f32[1023]{0:T(1024)} %param.9) | copy-start | bytes 12280
  9.1 3.8 %collective-permute-start.3 = (bf16[8,2048]{1,0:T(8,128)(2,1)S(1)}, bf16[8,2048]{1,0:T(8,128)(2,1)S(1)}, u32[]{:S(2)}, u32[]{:S(2)}) collective-permute-start(bf16[8,2048]{1,0:T(8,128)(2,1)S(1)} %get-tuple-element.18), channel_id=1, source_target_pairs={{0,3},{1,2},{2,1},{3,0},{4,7},{5,6},{6,5},{7,4},{8,11},{9,10},{10,... | collective-permute-start | bytes 98312 | tf_op jit(solution)/shard_map/ppermute | solution.py:278
  9.8 3.9 %collective-permute-start.4 = (bf16[8,2048]{1,0:T(8,128)(2,1)S(1)}, bf16[8,2048]{1,0:T(8,128)(2,1)S(1)}, u32[]{:S(2)}, u32[]{:S(2)}) collective-permute-start(bf16[8,2048]{1,0:T(8,128)(2,1)S(1)} %get-tuple-element.19), channel_id=1, source_target_pairs={{0,2},{1,3},{2,0},{3,1},{4,6},{5,7},{6,4},{7,5},{8,10},{9,11},{10,... | collective-permute-start | bytes 98312 | tf_op jit(solution)/shard_map/ppermute | solution.py:278
  10.6 3.2 %collective-permute-start.5 = (bf16[8,2048]{1,0:T(8,128)(2,1)S(1)}, bf16[8,2048]{1,0:T(8,128)(2,1)S(1)}, u32[]{:S(2)}, u32[]{:S(2)}) collective-permute-start(bf16[8,2048]{1,0:T(8,128)(2,1)S(1)} %get-tuple-element.20), channel_id=1, source_target_pairs={{0,1},{1,0},{2,3},{3,2},{4,5},{5,4},{6,7},{7,6},{8,9},{9,8},{10,11... | collective-permute-start | bytes 98312 | tf_op jit(solution)/shard_map/ppermute | solution.py:278
  13.8 5.0 %collective-permute-start.6 = (bf16[8,2048]{1,0:T(8,128)(2,1)S(1)}, bf16[8,2048]{1,0:T(8,128)(2,1)S(1)}, u32[]{:S(2)}, u32[]{:S(2)}) collective-permute-start(bf16[8,2048]{1,0:T(8,128)(2,1)S(1)} %get-tuple-element.22), channel_id=1, source_target_pairs={{0,12},{4,8},{8,4},{12,0},{16,28},{20,24},{24,20},{28,16},{1,13},{... | collective-permute-start | bytes 98312 | tf_op jit(solution)/shard_map/ppermute | solution.py:278
  16.4 3.9 %collective-permute-start.7 = (bf16[8,2048]{1,0:T(8,128)(2,1)S(1)}, bf16[8,2048]{1,0:T(8,128)(2,1)S(1)}, u32[]{:S(2)}, u32[]{:S(2)}) collective-permute-start(bf16[8,2048]{1,0:T(8,128)(2,1)S(1)} %get-tuple-element.22), channel_id=1, source_target_pairs={{0,8},{4,12},{8,0},{12,4},{16,24},{20,28},{24,16},{28,20},{1,9},{5... | collective-permute-start | bytes 98312 | tf_op jit(solution)/shard_map/ppermute | solution.py:278
  16.8 3.9 %collective-permute-start.8 = (bf16[8,2048]{1,0:T(8,128)(2,1)S(1)}, bf16[8,2048]{1,0:T(8,128)(2,1)S(1)}, u32[]{:S(2)}, u32[]{:S(2)}) collective-permute-start(bf16[8,2048]{1,0:T(8,128)(2,1)S(1)} %get-tuple-element.22), channel_id=1, source_target_pairs={{0,4},{4,0},{8,12},{12,8},{16,20},{20,16},{24,28},{28,24},{1,5},{5... | collective-permute-start | bytes 98312 | tf_op jit(solution)/shard_map/ppermute | solution.py:278
  21.0 4.9 %collective-permute-start.9 = (bf16[8,2048]{1,0:T(8,128)(2,1)S(1)}, bf16[8,2048]{1,0:T(8,128)(2,1)S(1)}, u32[]{:S(2)}, u32[]{:S(2)}) collective-permute-start(bf16[8,2048]{1,0:T(8,128)(2,1)S(1)} %get-tuple-element.24), channel_id=1, source_target_pairs={{0,16},{4,20},{8,24},{12,28},{16,0},{20,4},{24,8},{28,12},{1,17},{... | collective-permute-start | bytes 98312 | tf_op jit(solution)/shard_map/ppermute | solution.py:278

commit v3 on v2

--- a/solution.py
+++ b/solution.py
@@ -206,19 +206,17 @@
 
 
 def gather_kernel(taps_ref, *refs):
-    *parts, total_ref, low_ref = refs
+    *parts, low_ref = refs
     del taps_ref
-    total = sum(r[...].astype(jnp.float32) for r in parts)
-    total_ref[...] = total
-    low_ref[...] = total.astype(low_ref.dtype)
+    low_ref[...] = sum(r[...].astype(jnp.float32) for r in parts).astype(low_ref.dtype)
 
 
 def add_zones(taps, parts):
     return pl.pallas_call(
         gather_kernel,
-        out_shape=[jax.ShapeDtypeStruct(parts[0].shape, d) for d in (jnp.float32, jnp.bfloat16)],
+        out_shape=jax.ShapeDtypeStruct(parts[0].shape, jnp.bfloat16),
         in_specs=[VMEM] * (1 + len(parts)),
-        out_specs=[VMEM] * 2,
+        out_specs=VMEM,
         compiler_params=pltpu.CompilerParams(vmem_limit_bytes=LIMIT),
         name="add_zones",
     )(taps, *parts)
@@ -227,11 +225,13 @@
 def filter_kernel(near, taps_ref, *refs):
     values, outs = refs[:near], refs[near:]
     rows = values[0].shape[0]
-    values = [values[0], *values[:0:-1]]
-    together = jnp.concatenate([r[...].astype(jnp.float32) for r in values], axis=0)
+    together = jnp.concatenate([r[...] for r in values[::-1]], axis=0)
+    high = taps_ref[...].astype(jnp.bfloat16)
+    low = (taps_ref[...] - high.astype(jnp.float32)).astype(jnp.bfloat16)
     result = jnp.dot(
-        taps_ref[...], together, precision=lax.Precision.HIGHEST, preferred_element_type=jnp.float32
-    )
+        jnp.concatenate([high, low], axis=0), together, preferred_element_type=jnp.float32
+    )
+    result = result[: high.shape[0]] + result[high.shape[0] :]
     if len(outs) == 1:
         outs[0][...] = result.astype(outs[0].dtype)
         return
@@ -240,7 +240,7 @@
 
 
 def time_filter(taps, values):
-    rows, cells = values[0].shape
+    rows, cells = values[-1].shape
     steps = taps.shape[0] // rows
     if steps <= DIRECT:
         outs = [
@@ -276,6 +276,16 @@
 
 def swap(value, axis, by):
     return lax.ppermute(value, axis, [(i, i ^ by) for i in range(lax.axis_size(axis))])
+
+
+def swap_both(value, tm_by, zone_by):
+    owners, zones = lax.axis_size("tm"), lax.axis_size("zone")
+    pairs = [
+        (t * zones + z, (t ^ tm_by) * zones + (z ^ zone_by))
+        for t in range(owners)
+        for z in range(zones)
+    ]
+    return lax.ppermute(value, ("tm", "zone"), pairs)
 
 
 def shards(source_field, remap_weights, block_columns, piece_sizes, filter_taps):
@@ -289,14 +299,15 @@
     held, turned = hold(remap_weights)
     sent = remap(where, block_columns.T, piece_sizes, xs, held, turned)
     taps = prepare(where, filter_taps, steps, near, rows)
-    summed, low = add_zones(
-        taps, [sent[0]] + [swap(sent[step], "zone", step) for step in range(zones - 1, 0, -1)]
-    )
-    others = [swap(low, "tm", n) for n in range(near - 1, 0, -1)]
-    parts = time_filter(taps, [summed] + others)
+    low = add_zones(
+        taps, [sent[0]] + [swap(sent[step], "zone", step) for step in range(1, zones)]
+    )
+    flip = 1 if steps <= DIRECT else 0
+    others = [swap_both(low, n, flip) for n in range(near - 1, 0, -1)]
+    parts = time_filter(taps, others + [swap(low, "zone", flip) if flip else low])
     if steps <= DIRECT:
-        last = [parts[0]] + [swap(parts[step], "tm", near * step) for step in range(1, steps)]
-        return add_up(last)
+        last = [swap_both(parts[step], near * step, flip) for step in range(steps - 1, 0, -1)]
+        return add_up(last + [swap(parts[0], "zone", flip)])
     groups = [list(range(side, owners, near)) for side in range(near)]
     parts = lax.all_to_all(
         parts[0].reshape(steps, rows, cells), "tm", 0, 0, axis_index_groups=groups

time: 26.7 us -> 25.1 us (0.940)
  waiting for transfers between devices: 9.09 us -> 7.71 us
    ppermute x10 -> x8, waiting for transfers between devices: 9.09 us -> 3.28 us  [swap(): lax.ppermute(value, axis, [(i, i ^ by) for i in range(lax.axis_size(axis))])]
    ppermute x10 -> x8, starting transfers between devices: 11.2 us -> 5.58 us  [swap(): lax.ppermute(value, axis, [(i, i ^ by) for i in range(lax.axis_size(axis))])]
    ppermute x0 -> x4, starting transfers between devices: none -> 5.57 us  [swap_both(): return lax.ppermute(value, ('tm', 'zone'), pairs)]
    ppermute x0 -> x4, waiting for transfers between devices: none -> 4.43 us  [swap_both(): return lax.ppermute(value, ('tm', 'zone'), pairs)]
  transfers between devices with their start and end apart: 10 -> 12, of which waited for: 7 -> 7; matrix products, arithmetic and copies ran while one was open for 0% -> 0% of each run, Pallas kernels for 9% -> 10%
where the time goes in v3:
time: 25.1 us; the launch traced here: 25 us
  starting transfers between devices  11.1 us (44%)
  waiting for transfers between devices  7.71 us (31%)
  Pallas kernels  5.08 us (20%)
  other arithmetic  0.95 us (4%)
    ppermute x8, starting transfers between devices, swap(): lax.ppermute(value, axis, [(i, i ^ by) for i in range(lax.axis_size(axis))])  5.58 us
    ppermute x4, starting transfers between devices, swap_both(): return lax.ppermute(value, ('tm', 'zone'), pairs)  5.57 us
    ppermute x4, waiting for transfers between devices, swap_both(): return lax.ppermute(value, ('tm', 'zone'), pairs)  4.43 us
    ppermute x8, waiting for transfers between devices, swap(): lax.ppermute(value, axis, [(i, i ^ by) for i in range(lax.axis_size(axis))])  3.28 us
    pallas_call x1, Pallas kernels, hold(): pl.pallas_call(hold_kernel, out_shape=[jax.ShapeDtypeStruct((count, *weig...  2.23 us
    pallas_call x1, Pallas kernels, remap(): pl.pallas_call(functools.partial(remap_kernel, zones), out_shape=outs, in...  1.82 us
    convert_element_type x1, other arithmetic, shards(): xlow = source_field.astype(jnp.bfloat16)  0.87 us
    pallas_call x1, Pallas kernels, add_up(): pl.pallas_call(sum_kernel, out_shape=jax.ShapeDtypeStruct(parts[0].shape,...  0.64 us
  transfers between devices with their start and end apart: 12, of which 7 were waited for; matrix products, arithmetic and copies ran while one was open for 0% of the time, Pallas kernels for 10%

profile of v3, /device:TPU:0, one launch (start us, length us, event | category | flops | bytes accessed | tf_op | source)
XLA Modules:
  0.0 25.0 jit_solution(7232178990571296871)
XLA Ops:
  0.0 0.9 %convert_element_type.3.refs_0_ = bf16[8,2048]{1,0:T(8,128)(2,1)S(1)} convert(f32[8,2048]{1,0:T(8,128)} %param.5) | non-fusion elementwise | flops 16384 | bytes 98304 | tf_op jit(solution)/shard_map/convert_element_type | solution.py:297
  0.9 2.4 %collective-permute-start = (bf16[8,2048]{1,0:T(8,128)(2,1)S(1)}, bf16[8,2048]{1,0:T(8,128)(2,1)S(1)}, u32[]{:S(2)}, u32[]{:S(2)}) collective-permute-start(bf16[8,2048]{1,0:T(8,128)(2,1)S(1)} %convert_element_type.3.refs_0_), channel_id=1, source_target_pairs={{0,3},{1,2},{2,1},{3,0},{4,7},{5,6},{6,5},{7,4},{8,11},{9,10},{10,... | collective-permute-start | bytes 98312 | tf_op jit(solution)/shard_map/ppermute | solution.py:278
  3.3 0.6 %collective-permute-start.1 = (bf16[8,2048]{1,0:T(8,128)(2,1)S(1)}, bf16[8,2048]{1,0:T(8,128)(2,1)S(1)}, u32[]{:S(2)}, u32[]{:S(2)}) collective-permute-start(bf16[8,2048]{1,0:T(8,128)(2,1)S(1)} %convert_element_type.3.refs_0_), channel_id=1, source_target_pairs={{0,2},{1,3},{2,0},{3,1},{4,6},{5,7},{6,4},{7,5},{8,10},{9,11},{10,... | collective-permute-start | bytes 98312 | tf_op jit(solution)/shard_map/ppermute | solution.py:278
  3.8 0.1 collective-permute-start.2
  4.0 2.2 %hold.1 = (bf16[16,8,128,128]{3,2,1,0:T(8,128)(2,1)S(1)}, bf16[12,8,128,128]{3,2,1,0:T(8,128)(2,1)S(1)}) custom-call(bf16[16,8,128,128]{3,2,1,0:T(8,128)(2,1)} %weights_ref.1), custom_call_target="tpu_custom_call" | custom-call | bytes 8388608 | tf_op jit(solution)/shard_map/hold/pallas_call | solution.py:51
  6.3 1.0 %collective-permute-done.1.refs_2_ = bf16[8,2048]{1,0:T(8,128)(2,1)S(1)} collective-permute-done((bf16[8,2048]{1,0:T(8,128)(2,1)S(1)}, bf16[8,2048]{1,0:T(8,128)(2,1)S(1)}, u32[]{:S(2)}, u32[]{:S(2)}) %collective-permute-start.1) | collective-permute-done | bytes 32800 | tf_op jit(solution)/shard_map/ppermute | solution.py:278
  7.2 1.8 %remap.1 = (f32[8,2048]{1,0:T(8,128)S(1)}, bf16[8,2048]{1,0:T(8,128)(2,1)S(1)}, bf16[8,2048]{1,0:T(8,128)(2,1)S(1)}, bf16[8,2048]{1,0:T(8,128)(2,1)S(1)}) custom-call(s32[1,2]{1,0:T(1,128)S(1)} %add_bitcast_fusion.where_ref, s32[8,16]{1,0:T(8,128)S(1)} %bitcast.6, s32[1,8]{1,0:T(1,128)S(1)} %copy-done.2, bf16[8,2048]{1,0:T(8,128)(2,1)S(1)} %convert_element_type.3.refs_0_, ...), custom_call_target="tpu_custom_call" | custom-call | flops 100000000 | bytes 8388608 | tf_op jit(solution)/shard_map/remap/pallas_call | solution.py:193
  9.1 1.1 %collective-permute-start.4 = (bf16[8,2048]{1,0:T(8,128)(2,1)S(1)}, bf16[8,2048]{1,0:T(8,128)(2,1)S(1)}, u32[]{:S(2)}, u32[]{:S(2)}) collective-permute-start(bf16[8,2048]{1,0:T(8,128)(2,1)S(1)} %get-tuple-element.17), channel_id=1, source_target_pairs={{0,2},{1,3},{2,0},{3,1},{4,6},{5,7},{6,4},{7,5},{8,10},{9,11},{10,... | collective-permute-start | bytes 98312 | tf_op jit(solution)/shard_map/ppermute | solution.py:278
  10.2 0.8 %collective-permute-start.5 = (bf16[8,2048]{1,0:T(8,128)(2,1)S(1)}, bf16[8,2048]{1,0:T(8,128)(2,1)S(1)}, u32[]{:S(2)}, u32[]{:S(2)}) collective-permute-start(bf16[8,2048]{1,0:T(8,128)(2,1)S(1)} %get-tuple-element.18), channel_id=1, source_target_pairs={{0,3},{1,2},{2,1},{3,0},{4,7},{5,6},{6,5},{7,4},{8,11},{9,10},{10,... | collective-permute-start | bytes 98312 | tf_op jit(solution)/shard_map/ppermute | solution.py:278
  11.0 0.2 prepare.1.taps_ref
  11.3 1.9 %collective-permute-done.4.refs_2_ = bf16[8,2048]{1,0:T(8,128)(2,1)S(1)} collective-permute-done((bf16[8,2048]{1,0:T(8,128)(2,1)S(1)}, bf16[8,2048]{1,0:T(8,128)(2,1)S(1)}, u32[]{:S(2)}, u32[]{:S(2)}) %collective-permute-start.4) | collective-permute-done | bytes 32800 | tf_op jit(solution)/shard_map/ppermute | solution.py:278
  13.1 0.4 %collective-permute-done.5.refs_3_ = bf16[8,2048]{1,0:T(8,128)(2,1)S(1)} collective-permute-done((bf16[8,2048]{1,0:T(8,128)(2,1)S(1)}, bf16[8,2048]{1,0:T(8,128)(2,1)S(1)}, u32[]{:S(2)}, u32[]{:S(2)}) %collective-permute-start.5) | collective-permute-done | bytes 32800 | tf_op jit(solution)/shard_map/ppermute | solution.py:278
  13.6 2.4 %collective-permute-start.6 = (bf16[8,2048]{1,0:T(8,128)(2,1)S(1)}, bf16[8,2048]{1,0:T(8,128)(2,1)S(1)}, u32[]{:S(2)}, u32[]{:S(2)}) collective-permute-start(bf16[8,2048]{1,0:T(8,128)(2,1)S(1)} %add_zones.1), channel_id=1, source_target_pairs={{0,13},{1,12},{2,15},{3,14},{4,9},{5,8},{6,11},{7,10},{8,5},{9,4},... | collective-permute-start | bytes 98312 | tf_op jit(solution)/shard_map/ppermute | solution.py:288
  16.0 0.4 %collective-permute-start.7 = (bf16[8,2048]{1,0:T(8,128)(2,1)S(1)}, bf16[8,2048]{1,0:T(8,128)(2,1)S(1)}, u32[]{:S(2)}, u32[]{:S(2)}) collective-permute-start(bf16[8,2048]{1,0:T(8,128)(2,1)S(1)} %add_zones.1), channel_id=1, source_target_pairs={{0,9},{1,8},{2,11},{3,10},{4,13},{5,12},{6,15},{7,14},{8,1},{9,0},... | collective-permute-start | bytes 98312 | tf_op jit(solution)/shard_map/ppermute | solution.py:288
  16.4 0.3 %collective-permute-start.8 = (bf16[8,2048]{1,0:T(8,128)(2,1)S(1)}, bf16[8,2048]{1,0:T(8,128)(2,1)S(1)}, u32[]{:S(2)}, u32[]{:S(2)}) collective-permute-start(bf16[8,2048]{1,0:T(8,128)(2,1)S(1)} %add_zones.1), channel_id=1, source_target_pairs={{0,5},{1,4},{2,7},{3,6},{4,1},{5,0},{6,3},{7,2},{8,13},{9,12},{10,... | collective-permute-start | bytes 98312 | tf_op jit(solution)/shard_map/ppermute | solution.py:288
  16.6 0.4 %collective-permute-start.9 = (bf16[8,2048]{1,0:T(8,128)(2,1)S(1)}, bf16[8,2048]{1,0:T(8,128)(2,1)S(1)}, u32[]{:S(2)}, u32[]{:S(2)}) collective-permute-start(bf16[8,2048]{1,0:T(8,128)(2,1)S(1)} %add_zones.1), channel_id=1, source_target_pairs={{0,1},{1,0},{2,3},{3,2},{4,5},{5,4},{6,7},{7,6},{8,9},{9,8},{10,11... | collective-permute-start | bytes 98312 | tf_op jit(solution)/shard_map/ppermute | solution.py:278
  17.0 0.9 %collective-permute-done.6.refs_0_ = bf16[8,2048]{1,0:T(8,128)(2,1)S(1)} collective-permute-done((bf16[8,2048]{1,0:T(8,128)(2,1)S(1)}, bf16[8,2048]{1,0:T(8,128)(2,1)S(1)}, u32[]{:S(2)}, u32[]{:S(2)}) %collective-permute-start.6) | collective-permute-done | bytes 32800 | tf_op jit(solution)/shard_map/ppermute | solution.py:288
  17.9 1.4 %collective-permute-done.7.refs_1_ = bf16[8,2048]{1,0:T(8,128)(2,1)S(1)} collective-permute-done((bf16[8,2048]{1,0:T(8,128)(2,1)S(1)}, bf16[8,2048]{1,0:T(8,128)(2,1)S(1)}, u32[]{:S(2)}, u32[]{:S(2)}) %collective-permute-start.7) | collective-permute-done | bytes 32800 | tf_op jit(solution)/shard_map/ppermute | solution.py:288
  19.3 0.4 %collective-permute-done.8.refs_2_ = bf16[8,2048]{1,0:T(8,128)(2,1)S(1)} collective-permute-done((bf16[8,2048]{1,0:T(8,128)(2,1)S(1)}, bf16[8,2048]{1,0:T(8,128)(2,1)S(1)}, u32[]{:S(2)}, u32[]{:S(2)}) %collective-permute-start.8) | collective-permute-done | bytes 32800 | tf_op jit(solution)/shard_map/ppermute | solution.py:288
  19.7 0.1 time_filter.1
  19.9 0.2 collective-permute-start.11
  20.1 2.5 %collective-permute-start.10 = (bf16[8,2048]{1,0:T(8,128)(2,1)S(1)}, bf16[8,2048]{1,0:T(8,128)(2,1)S(1)}, u32[]{:S(2)}, u32[]{:S(2)}) collective-permute-start(bf16[8,2048]{1,0:T(8,128)(2,1)S(1)} %get-tuple-element.19), channel_id=1, source_target_pairs={{0,17},{1,16},{2,19},{3,18},{4,21},{5,20},{6,23},{7,22},{8,25},{9,... | collective-permute-start | bytes 98312 | tf_op jit(solution)/shard_map/ppermute | solution.py:288
  22.6 1.7 %collective-permute-done.10.refs_0_ = bf16[8,2048]{1,0:T(8,128)(2,1)S(1)} collective-permute-done((bf16[8,2048]{1,0:T(8,128)(2,1)S(1)}, bf16[8,2048]{1,0:T(8,128)(2,1)S(1)}, u32[]{:S(2)}, u32[]{:S(2)}) %collective-permute-start.10) | collective-permute-done | bytes 32800 | tf_op jit(solution)/shard_map/ppermute | solution.py:288
  24.3 0.6 %add_up.1 = f32[8,2048]{1,0:T(8,128)} custom-call(bf16[8,2048]{1,0:T(8,128)(2,1)S(1)} %collective-permute-done.10.refs_0_, f32[8,2048]{1,0:T(8,128)S(1)} %collective-permute-done.11.refs_1_), custom_call_target="tpu_custom_call" | custom-call | tf_op jit(solution)/shard_map/add_up/pallas_call | solution.py:267
  (14 shorter events, 0.2 us)
Async XLA Ops:
  0.0 7.2 %copy-start = (s32[16,8]{0,1:T(8,128)S(1)}, s32[16,8]{0,1:T(8,128)}, u32[]{:S(2)}) copy-start(s32[16,8]{0,1:T(8,128)} %param.7) | copy-start | bytes 1540
  0.0 7.2 %copy-start.2 = (s32[1,8]{1,0:T(1,128)S(1)}, s32[1,8]{1,0:T(1,128)}, u32[]{:S(2)}) copy-start(s32[1,8]{1,0:T(1,128)} %sizes_ref.1) | copy-start | bytes 100
  0.9 5.4 %collective-permute-start = (bf16[8,2048]{1,0:T(8,128)(2,1)S(1)}, bf16[8,2048]{1,0:T(8,128)(2,1)S(1)}, u32[]{:S(2)}, u32[]{:S(2)}) collective-permute-start(bf16[8,2048]{1,0:T(8,128)(2,1)S(1)} %convert_element_type.3.refs_0_), channel_id=1, source_target_pairs={{0,3},{1,2},{2,1},{3,0},{4,7},{5,6},{6,5},{7,4},{8,11},{9,10},{10,... | collective-permute-start | bytes 98312 | tf_op jit(solution)/shard_map/ppermute | solution.py:278
  3.3 4.0 %collective-permute-start.1 = (bf16[8,2048]{1,0:T(8,128)(2,1)S(1)}, bf16[8,2048]{1,0:T(8,128)(2,1)S(1)}, u32[]{:S(2)}, u32[]{:S(2)}) collective-permute-start(bf16[8,2048]{1,0:T(8,128)(2,1)S(1)} %convert_element_type.3.refs_0_), channel_id=1, source_target_pairs={{0,2},{1,3},{2,0},{3,1},{4,6},{5,7},{6,4},{7,5},{8,10},{9,11},{10,... | collective-permute-start | bytes 98312 | tf_op jit(solution)/shard_map/ppermute | solution.py:278
  3.8 3.4 %collective-permute-start.2 = (bf16[8,2048]{1,0:T(8,128)(2,1)S(1)}, bf16[8,2048]{1,0:T(8,128)(2,1)S(1)}, u32[]{:S(2)}, u32[]{:S(2)}) collective-permute-start(bf16[8,2048]{1,0:T(8,128)(2,1)S(1)} %convert_element_type.3.refs_0_), channel_id=1, source_target_pairs={{0,1},{1,0},{2,3},{3,2},{4,5},{5,4},{6,7},{7,6},{8,9},{9,8},{10,11... | collective-permute-start | bytes 98312 | tf_op jit(solution)/shard_map/ppermute | solution.py:278
  6.3 4.8 %copy-start.1 = (f32[1023]{0:T(1024)S(1)}, f32[1023]{0:T(1024)}, u32[]{:S(2)}) copy-start(f32[1023]{0:T(1024)} %param.9) | copy-start | bytes 12280
  9.1 2.2 %collective-permute-start.3 = (bf16[8,2048]{1,0:T(8,128)(2,1)S(1)}, bf16[8,2048]{1,0:T(8,128)(2,1)S(1)}, u32[]{:S(2)}, u32[]{:S(2)}) collective-permute-start(bf16[8,2048]{1,0:T(8,128)(2,1)S(1)} %get-tuple-element.16), channel_id=1, source_target_pairs={{0,1},{1,0},{2,3},{3,2},{4,5},{5,4},{6,7},{7,6},{8,9},{9,8},{10,11... | collective-permute-start | bytes 98312 | tf_op jit(solution)/shard_map/ppermute | solution.py:278
  9.1 4.0 %collective-permute-start.4 = (bf16[8,2048]{1,0:T(8,128)(2,1)S(1)}, bf16[8,2048]{1,0:T(8,128)(2,1)S(1)}, u32[]{:S(2)}, u32[]{:S(2)}) collective-permute-start(bf16[8,2048]{1,0:T(8,128)(2,1)S(1)} %get-tuple-element.17), channel_id=1, source_target_pairs={{0,2},{1,3},{2,0},{3,1},{4,6},{5,7},{6,4},{7,5},{8,10},{9,11},{10,... | collective-permute-start | bytes 98312 | tf_op jit(solution)/shard_map/ppermute | solution.py:278
  10.2 3.4 %collective-permute-start.5 = (bf16[8,2048]{1,0:T(8,128)(2,1)S(1)}, bf16[8,2048]{1,0:T(8,128)(2,1)S(1)}, u32[]{:S(2)}, u32[]{:S(2)}) collective-permute-start(bf16[8,2048]{1,0:T(8,128)(2,1)S(1)} %get-tuple-element.18), channel_id=1, source_target_pairs={{0,3},{1,2},{2,1},{3,0},{4,7},{5,6},{6,5},{7,4},{8,11},{9,10},{10,... | collective-permute-start | bytes 98312 | tf_op jit(solution)/shard_map/ppermute | solution.py:278
  13.6 4.3 %collective-permute-start.6 = (bf16[8,2048]{1,0:T(8,128)(2,1)S(1)}, bf16[8,2048]{1,0:T(8,128)(2,1)S(1)}, u32[]{:S(2)}, u32[]{:S(2)}) collective-permute-start(bf16[8,2048]{1,0:T(8,128)(2,1)S(1)} %add_zones.1), channel_id=1, source_target_pairs={{0,13},{1,12},{2,15},{3,14},{4,9},{5,8},{6,11},{7,10},{8,5},{9,4},... | collective-permute-start | bytes 98312 | tf_op jit(solution)/shard_map/ppermute | solution.py:288
  16.0 3.3 %collective-permute-start.7 = (bf16[8,2048]{1,0:T(8,128)(2,1)S(1)}, bf16[8,2048]{1,0:T(8,128)(2,1)S(1)}, u32[]{:S(2)}, u32[]{:S(2)}) collective-permute-start(bf16[8,2048]{1,0:T(8,128)(2,1)S(1)} %add_zones.1), channel_id=1, source_target_pairs={{0,9},{1,8},{2,11},{3,10},{4,13},{5,12},{6,15},{7,14},{8,1},{9,0},... | collective-permute-start | bytes 98312 | tf_op jit(solution)/shard_map/ppermute | solution.py:288
  16.4 3.3 %collective-permute-start.8 = (bf16[8,2048]{1,0:T(8,128)(2,1)S(1)}, bf16[8,2048]{1,0:T(8,128)(2,1)S(1)}, u32[]{:S(2)}, u32[]{:S(2)}) collective-permute-start(bf16[8,2048]{1,0:T(8,128)(2,1)S(1)} %add_zones.1), channel_id=1, source_target_pairs={{0,5},{1,4},{2,7},{3,6},{4,1},{5,0},{6,3},{7,2},{8,13},{9,12},{10,... | collective-permute-start | bytes 98312 | tf_op jit(solution)/shard_map/ppermute | solution.py:288
  16.6 3.1 %collective-permute-start.9 = (bf16[8,2048]{1,0:T(8,128)(2,1)S(1)}, bf16[8,2048]{1,0:T(8,128)(2,1)S(1)}, u32[]{:S(2)}, u32[]{:S(2)}) collective-permute-start(bf16[8,2048]{1,0:T(8,128)(2,1)S(1)} %add_zones.1), channel_id=1, source_target_pairs={{0,1},{1,0},{2,3},{3,2},{4,5},{5,4},{6,7},{7,6},{8,9},{9,8},{10,11... | collective-permute-start | bytes 98312 | tf_op jit(solution)/shard_map/ppermute | solution.py:278
  19.9 4.5 %collective-permute-start.11 = (f32[8,2048]{1,0:T(8,128)S(1)}, f32[8,2048]{1,0:T(8,128)S(1)}, u32[]{:S(2)}, u32[]{:S(2)}) collective-permute-start(f32[8,2048]{1,0:T(8,128)S(1)} %get-tuple-element.20), channel_id=1, source_target_pairs={{0,1},{1,0},{2,3},{3,2},{4,5},{5,4},{6,7},{7,6},{8,9},{9,8},{10,11... | collective-permute-start | bytes 196616 | tf_op jit(solution)/shard_map/ppermute | solution.py:278
  20.1 4.2 %collective-permute-start.10 = (bf16[8,2048]{1,0:T(8,128)(2,1)S(1)}, bf16[8,2048]{1,0:T(8,128)(2,1)S(1)}, u32[]{:S(2)}, u32[]{:S(2)}) collective-permute-start(bf16[8,2048]{1,0:T(8,128)(2,1)S(1)} %get-tuple-element.19), channel_id=1, source_target_pairs={{0,17},{1,16},{2,19},{3,18},{4,21},{5,20},{6,23},{7,22},{8,25},{9,... | collective-permute-start | bytes 98312 | tf_op jit(solution)/shard_map/ppermute | solution.py:288

commit v4 on v3

--- a/solution.py
+++ b/solution.py
@@ -12,14 +12,6 @@
 LIMIT = 16 * 2**20
 DIRECT = 8
 NEAR = 4
-
-
-def three_parts(value):
-    high = value.astype(jnp.bfloat16)
-    rest = value - high.astype(jnp.float32)
-    middle = rest.astype(jnp.bfloat16)
-    low = (rest - middle.astype(jnp.float32)).astype(jnp.bfloat16)
-    return high, middle, low
 
 
 def ahead(snapshots, half_width, width):
@@ -135,30 +127,31 @@
             wide = jnp.concatenate([weights_ref[i, k] for k in range(slots)], axis=1)
             wind = lax.dot_general(picked, wide, NT, preferred_element_type=jnp.float32)
         pieces.append(wind * jnp.abs(wind))
-    stress = jnp.concatenate(pieces, axis=1)
-
-    basins, cells = sizes_ref.shape[1], x_refs[0].shape[1]
-    cell_ids = lax.broadcasted_iota(jnp.int32, (1, cells), 1)
-    basin_ids = jnp.zeros((1, cells), jnp.int32)
-    basin_lanes = lax.broadcasted_iota(jnp.int32, (1, basins), 1)
-    counts = jnp.zeros((1, basins), jnp.int32)
-    end = 0
-    for g in range(basins):
-        counts = jnp.where(basin_lanes == g, sizes_ref[0, g], counts)
-        if g:
-            basin_ids += (cell_ids >= end).astype(jnp.int32)
-        end = end + sizes_ref[0, g]
-    member = lax.broadcasted_iota(jnp.int32, (basins, cells), 0) == basin_ids
-    member = member.astype(jnp.float32).astype(jnp.bfloat16)
-    parts = lax.dot_general(
-        jnp.concatenate(three_parts(stress), axis=0), member, NT, preferred_element_type=jnp.float32
-    )
-    totals = parts[:rows] + parts[rows : 2 * rows] + parts[2 * rows :]
-    means = totals / counts.astype(jnp.float32)
-    spread = jnp.dot(
-        jnp.concatenate(three_parts(means), axis=0), member, preferred_element_type=jnp.float32
-    )
-    anomaly = stress - (spread[:rows] + spread[rows : 2 * rows] + spread[2 * rows :])
+    cell_ids = lax.broadcasted_iota(jnp.int32, (rows, size), 1)
+    ends = [0]
+    for g in range(sizes_ref.shape[1]):
+        ends.append(ends[-1] + sizes_ref[0, g])
+    totals = [jnp.zeros((rows, size), jnp.float32)] * sizes_ref.shape[1]
+    for i, stress in enumerate(pieces):
+        ids = cell_ids + i * size
+        for g, total in enumerate(totals):
+            inside = (ids >= ends[g]) & (ids < ends[g + 1])
+            totals[g] = total + jnp.where(inside, stress, 0.0)
+    means = [
+        jnp.broadcast_to(
+            jnp.sum(total, axis=1, keepdims=True) / sizes_ref[0, g].astype(jnp.float32),
+            (rows, size),
+        )
+        for g, total in enumerate(totals)
+    ]
+    anomalies = []
+    for i, stress in enumerate(pieces):
+        ids = cell_ids + i * size
+        spread = means[0]
+        for g in range(1, len(means)):
+            spread = jnp.where(ids >= ends[g], means[g], spread)
+        anomalies.append(stress - spread)
+    anomaly = jnp.concatenate(anomalies, axis=1)
 
     high = anomaly.astype(jnp.bfloat16)
     low = (anomaly - high.astype(jnp.float32)).astype(jnp.bfloat16)

time: 25.1 us -> 25 us (level)
  no operation moved by 1% of the time
where the time goes in v4:
time: 25 us; the launch traced here: 24.8 us
  starting transfers between devices  11.1 us (44%)
  waiting for transfers between devices  7.7 us (31%)
  Pallas kernels  4.91 us (20%)
  other arithmetic  0.95 us (4%)
    ppermute x4, starting transfers between devices, swap_both(): return lax.ppermute(value, ('tm', 'zone'), pairs)  5.58 us
    ppermute x8, starting transfers between devices, swap(): lax.ppermute(value, axis, [(i, i ^ by) for i in range(lax.axis_size(axis))])  5.57 us
    ppermute x4, waiting for transfers between devices, swap_both(): return lax.ppermute(value, ('tm', 'zone'), pairs)  4.42 us
    ppermute x8, waiting for transfers between devices, swap(): lax.ppermute(value, axis, [(i, i ^ by) for i in range(lax.axis_size(axis))])  3.28 us
    pallas_call x1, Pallas kernels, hold(): pl.pallas_call(hold_kernel, out_shape=[jax.ShapeDtypeStruct((count, *weig...  2.23 us
    pallas_call x1, Pallas kernels, remap(): pl.pallas_call(functools.partial(remap_kernel, zones), out_shape=outs, in...  1.65 us
    convert_element_type x1, other arithmetic, shards(): xlow = source_field.astype(jnp.bfloat16)  0.87 us
    pallas_call x1, Pallas kernels, add_up(): pl.pallas_call(sum_kernel, out_shape=jax.ShapeDtypeStruct(parts[0].shape,...  0.64 us
  transfers between devices with their start and end apart: 12, of which 7 were waited for; matrix products, arithmetic and copies ran while one was open for 0% of the time, Pallas kernels for 10%

profile of v4, /device:TPU:0, one launch (start us, length us, event | category | flops | bytes accessed | tf_op | source)
XLA Modules:
  0.0 24.8 jit_solution(1471142474175334394)
XLA Ops:
  0.0 0.9 %convert_element_type.3.refs_0_ = bf16[8,2048]{1,0:T(8,128)(2,1)S(1)} convert(f32[8,2048]{1,0:T(8,128)} %param.5) | non-fusion elementwise | flops 16384 | bytes 98304 | tf_op jit(solution)/shard_map/convert_element_type | solution.py:290
  0.9 2.4 %collective-permute-start = (bf16[8,2048]{1,0:T(8,128)(2,1)S(1)}, bf16[8,2048]{1,0:T(8,128)(2,1)S(1)}, u32[]{:S(2)}, u32[]{:S(2)}) collective-permute-start(bf16[8,2048]{1,0:T(8,128)(2,1)S(1)} %convert_element_type.3.refs_0_), channel_id=1, source_target_pairs={{0,3},{1,2},{2,1},{3,0},{4,7},{5,6},{6,5},{7,4},{8,11},{9,10},{10,... | collective-permute-start | bytes 98312 | tf_op jit(solution)/shard_map/ppermute | solution.py:271
  3.3 0.6 %collective-permute-start.1 = (bf16[8,2048]{1,0:T(8,128)(2,1)S(1)}, bf16[8,2048]{1,0:T(8,128)(2,1)S(1)}, u32[]{:S(2)}, u32[]{:S(2)}) collective-permute-start(bf16[8,2048]{1,0:T(8,128)(2,1)S(1)} %convert_element_type.3.refs_0_), channel_id=1, source_target_pairs={{0,2},{1,3},{2,0},{3,1},{4,6},{5,7},{6,4},{7,5},{8,10},{9,11},{10,... | collective-permute-start | bytes 98312 | tf_op jit(solution)/shard_map/ppermute | solution.py:271
  3.8 0.1 collective-permute-start.2
  4.0 2.2 %hold.1 = (bf16[16,8,128,128]{3,2,1,0:T(8,128)(2,1)S(1)}, bf16[12,8,128,128]{3,2,1,0:T(8,128)(2,1)S(1)}) custom-call(bf16[16,8,128,128]{3,2,1,0:T(8,128)(2,1)} %weights_ref.1), custom_call_target="tpu_custom_call" | custom-call | bytes 8388608 | tf_op jit(solution)/shard_map/hold/pallas_call | solution.py:43
  6.3 1.0 %collective-permute-done.1.refs_2_ = bf16[8,2048]{1,0:T(8,128)(2,1)S(1)} collective-permute-done((bf16[8,2048]{1,0:T(8,128)(2,1)S(1)}, bf16[8,2048]{1,0:T(8,128)(2,1)S(1)}, u32[]{:S(2)}, u32[]{:S(2)}) %collective-permute-start.1) | collective-permute-done | bytes 32800 | tf_op jit(solution)/shard_map/ppermute | solution.py:271
  7.2 1.6 %remap.1 = (f32[8,2048]{1,0:T(8,128)S(1)}, bf16[8,2048]{1,0:T(8,128)(2,1)S(1)}, bf16[8,2048]{1,0:T(8,128)(2,1)S(1)}, bf16[8,2048]{1,0:T(8,128)(2,1)S(1)}) custom-call(s32[1,2]{1,0:T(1,128)S(1)} %add_bitcast_fusion.where_ref, s32[8,16]{1,0:T(8,128)S(1)} %bitcast.6, s32[1,8]{1,0:T(1,128)S(1)} %copy-done.2, bf16[8,2048]{1,0:T(8,128)(2,1)S(1)} %convert_element_type.3.refs_0_, ...), custom_call_target="tpu_custom_call" | custom-call | flops 100000000 | bytes 8388608 | tf_op jit(solution)/shard_map/remap/pallas_call | solution.py:186
  9.0 1.1 %collective-permute-start.4 = (bf16[8,2048]{1,0:T(8,128)(2,1)S(1)}, bf16[8,2048]{1,0:T(8,128)(2,1)S(1)}, u32[]{:S(2)}, u32[]{:S(2)}) collective-permute-start(bf16[8,2048]{1,0:T(8,128)(2,1)S(1)} %get-tuple-element.17), channel_id=1, source_target_pairs={{0,2},{1,3},{2,0},{3,1},{4,6},{5,7},{6,4},{7,5},{8,10},{9,11},{10,... | collective-permute-start | bytes 98312 | tf_op jit(solution)/shard_map/ppermute | solution.py:271
  10.0 0.8 %collective-permute-start.5 = (bf16[8,2048]{1,0:T(8,128)(2,1)S(1)}, bf16[8,2048]{1,0:T(8,128)(2,1)S(1)}, u32[]{:S(2)}, u32[]{:S(2)}) collective-permute-start(bf16[8,2048]{1,0:T(8,128)(2,1)S(1)} %get-tuple-element.18), channel_id=1, source_target_pairs={{0,3},{1,2},{2,1},{3,0},{4,7},{5,6},{6,5},{7,4},{8,11},{9,10},{10,... | collective-permute-start | bytes 98312 | tf_op jit(solution)/shard_map/ppermute | solution.py:271
  10.8 0.2 prepare.1.taps_ref
  11.1 1.9 %collective-permute-done.4.refs_2_ = bf16[8,2048]{1,0:T(8,128)(2,1)S(1)} collective-permute-done((bf16[8,2048]{1,0:T(8,128)(2,1)S(1)}, bf16[8,2048]{1,0:T(8,128)(2,1)S(1)}, u32[]{:S(2)}, u32[]{:S(2)}) %collective-permute-start.4) | collective-permute-done | bytes 32800 | tf_op jit(solution)/shard_map/ppermute | solution.py:271
  13.0 0.4 %collective-permute-done.5.refs_3_ = bf16[8,2048]{1,0:T(8,128)(2,1)S(1)} collective-permute-done((bf16[8,2048]{1,0:T(8,128)(2,1)S(1)}, bf16[8,2048]{1,0:T(8,128)(2,1)S(1)}, u32[]{:S(2)}, u32[]{:S(2)}) %collective-permute-start.5) | collective-permute-done | bytes 32800 | tf_op jit(solution)/shard_map/ppermute | solution.py:271
  13.4 2.4 %collective-permute-start.6 = (bf16[8,2048]{1,0:T(8,128)(2,1)S(1)}, bf16[8,2048]{1,0:T(8,128)(2,1)S(1)}, u32[]{:S(2)}, u32[]{:S(2)}) collective-permute-start(bf16[8,2048]{1,0:T(8,128)(2,1)S(1)} %add_zones.1), channel_id=1, source_target_pairs={{0,13},{1,12},{2,15},{3,14},{4,9},{5,8},{6,11},{7,10},{8,5},{9,4},... | collective-permute-start | bytes 98312 | tf_op jit(solution)/shard_map/ppermute | solution.py:281
  15.8 0.4 %collective-permute-start.7 = (bf16[8,2048]{1,0:T(8,128)(2,1)S(1)}, bf16[8,2048]{1,0:T(8,128)(2,1)S(1)}, u32[]{:S(2)}, u32[]{:S(2)}) collective-permute-start(bf16[8,2048]{1,0:T(8,128)(2,1)S(1)} %add_zones.1), channel_id=1, source_target_pairs={{0,9},{1,8},{2,11},{3,10},{4,13},{5,12},{6,15},{7,14},{8,1},{9,0},... | collective-permute-start | bytes 98312 | tf_op jit(solution)/shard_map/ppermute | solution.py:281
  16.2 0.3 %collective-permute-start.8 = (bf16[8,2048]{1,0:T(8,128)(2,1)S(1)}, bf16[8,2048]{1,0:T(8,128)(2,1)S(1)}, u32[]{:S(2)}, u32[]{:S(2)}) collective-permute-start(bf16[8,2048]{1,0:T(8,128)(2,1)S(1)} %add_zones.1), channel_id=1, source_target_pairs={{0,5},{1,4},{2,7},{3,6},{4,1},{5,0},{6,3},{7,2},{8,13},{9,12},{10,... | collective-permute-start | bytes 98312 | tf_op jit(solution)/shard_map/ppermute | solution.py:281
  16.5 0.3 %collective-permute-start.9 = (bf16[8,2048]{1,0:T(8,128)(2,1)S(1)}, bf16[8,2048]{1,0:T(8,128)(2,1)S(1)}, u32[]{:S(2)}, u32[]{:S(2)}) collective-permute-start(bf16[8,2048]{1,0:T(8,128)(2,1)S(1)} %add_zones.1), channel_id=1, source_target_pairs={{0,1},{1,0},{2,3},{3,2},{4,5},{5,4},{6,7},{7,6},{8,9},{9,8},{10,11... | collective-permute-start | bytes 98312 | tf_op jit(solution)/shard_map/ppermute | solution.py:271
  16.8 0.9 %collective-permute-done.6.refs_0_ = bf16[8,2048]{1,0:T(8,128)(2,1)S(1)} collective-permute-done((bf16[8,2048]{1,0:T(8,128)(2,1)S(1)}, bf16[8,2048]{1,0:T(8,128)(2,1)S(1)}, u32[]{:S(2)}, u32[]{:S(2)}) %collective-permute-start.6) | collective-permute-done | bytes 32800 | tf_op jit(solution)/shard_map/ppermute | solution.py:281
  17.7 1.4 %collective-permute-done.7.refs_1_ = bf16[8,2048]{1,0:T(8,128)(2,1)S(1)} collective-permute-done((bf16[8,2048]{1,0:T(8,128)(2,1)S(1)}, bf16[8,2048]{1,0:T(8,128)(2,1)S(1)}, u32[]{:S(2)}, u32[]{:S(2)}) %collective-permute-start.7) | collective-permute-done | bytes 32800 | tf_op jit(solution)/shard_map/ppermute | solution.py:281
  19.1 0.4 %collective-permute-done.8.refs_2_ = bf16[8,2048]{1,0:T(8,128)(2,1)S(1)} collective-permute-done((bf16[8,2048]{1,0:T(8,128)(2,1)S(1)}, bf16[8,2048]{1,0:T(8,128)(2,1)S(1)}, u32[]{:S(2)}, u32[]{:S(2)}) %collective-permute-start.8) | collective-permute-done | bytes 32800 | tf_op jit(solution)/shard_map/ppermute | solution.py:281
  19.5 0.1 time_filter.1
  19.7 0.2 collective-permute-start.11
  19.9 2.5 %collective-permute-start.10 = (bf16[8,2048]{1,0:T(8,128)(2,1)S(1)}, bf16[8,2048]{1,0:T(8,128)(2,1)S(1)}, u32[]{:S(2)}, u32[]{:S(2)}) collective-permute-start(bf16[8,2048]{1,0:T(8,128)(2,1)S(1)} %get-tuple-element.19), channel_id=1, source_target_pairs={{0,17},{1,16},{2,19},{3,18},{4,21},{5,20},{6,23},{7,22},{8,25},{9,... | collective-permute-start | bytes 98312 | tf_op jit(solution)/shard_map/ppermute | solution.py:281
  22.5 1.7 %collective-permute-done.10.refs_0_ = bf16[8,2048]{1,0:T(8,128)(2,1)S(1)} collective-permute-done((bf16[8,2048]{1,0:T(8,128)(2,1)S(1)}, bf16[8,2048]{1,0:T(8,128)(2,1)S(1)}, u32[]{:S(2)}, u32[]{:S(2)}) %collective-permute-start.10) | collective-permute-done | bytes 32800 | tf_op jit(solution)/shard_map/ppermute | solution.py:281
  24.2 0.6 %add_up.1 = f32[8,2048]{1,0:T(8,128)} custom-call(bf16[8,2048]{1,0:T(8,128)(2,1)S(1)} %collective-permute-done.10.refs_0_, f32[8,2048]{1,0:T(8,128)S(1)} %collective-permute-done.11.refs_1_), custom_call_target="tpu_custom_call" | custom-call | tf_op jit(solution)/shard_map/add_up/pallas_call | solution.py:260
  (14 shorter events, 0.2 us)
Async XLA Ops:
  0.0 7.2 %copy-start = (s32[16,8]{0,1:T(8,128)S(1)}, s32[16,8]{0,1:T(8,128)}, u32[]{:S(2)}) copy-start(s32[16,8]{0,1:T(8,128)} %param.7) | copy-start | bytes 1540
  0.0 7.2 %copy-start.2 = (s32[1,8]{1,0:T(1,128)S(1)}, s32[1,8]{1,0:T(1,128)}, u32[]{:S(2)}) copy-start(s32[1,8]{1,0:T(1,128)} %sizes_ref.1) | copy-start | bytes 100
  0.9 5.4 %collective-permute-start = (bf16[8,2048]{1,0:T(8,128)(2,1)S(1)}, bf16[8,2048]{1,0:T(8,128)(2,1)S(1)}, u32[]{:S(2)}, u32[]{:S(2)}) collective-permute-start(bf16[8,2048]{1,0:T(8,128)(2,1)S(1)} %convert_element_type.3.refs_0_), channel_id=1, source_target_pairs={{0,3},{1,2},{2,1},{3,0},{4,7},{5,6},{6,5},{7,4},{8,11},{9,10},{10,... | collective-permute-start | bytes 98312 | tf_op jit(solution)/shard_map/ppermute | solution.py:271
  3.3 4.0 %collective-permute-start.1 = (bf16[8,2048]{1,0:T(8,128)(2,1)S(1)}, bf16[8,2048]{1,0:T(8,128)(2,1)S(1)}, u32[]{:S(2)}, u32[]{:S(2)}) collective-permute-start(bf16[8,2048]{1,0:T(8,128)(2,1)S(1)} %convert_element_type.3.refs_0_), channel_id=1, source_target_pairs={{0,2},{1,3},{2,0},{3,1},{4,6},{5,7},{6,4},{7,5},{8,10},{9,11},{10,... | collective-permute-start | bytes 98312 | tf_op jit(solution)/shard_map/ppermute | solution.py:271
  3.8 3.4 %collective-permute-start.2 = (bf16[8,2048]{1,0:T(8,128)(2,1)S(1)}, bf16[8,2048]{1,0:T(8,128)(2,1)S(1)}, u32[]{:S(2)}, u32[]{:S(2)}) collective-permute-start(bf16[8,2048]{1,0:T(8,128)(2,1)S(1)} %convert_element_type.3.refs_0_), channel_id=1, source_target_pairs={{0,1},{1,0},{2,3},{3,2},{4,5},{5,4},{6,7},{7,6},{8,9},{9,8},{10,11... | collective-permute-start | bytes 98312 | tf_op jit(solution)/shard_map/ppermute | solution.py:271
  6.3 4.6 %copy-start.1 = (f32[1023]{0:T(1024)S(1)}, f32[1023]{0:T(1024)}, u32[]{:S(2)}) copy-start(f32[1023]{0:T(1024)} %param.9) | copy-start | bytes 12280
  8.9 2.2 %collective-permute-start.3 = (bf16[8,2048]{1,0:T(8,128)(2,1)S(1)}, bf16[8,2048]{1,0:T(8,128)(2,1)S(1)}, u32[]{:S(2)}, u32[]{:S(2)}) collective-permute-start(bf16[8,2048]{1,0:T(8,128)(2,1)S(1)} %get-tuple-element.16), channel_id=1, source_target_pairs={{0,1},{1,0},{2,3},{3,2},{4,5},{5,4},{6,7},{7,6},{8,9},{9,8},{10,11... | collective-permute-start | bytes 98312 | tf_op jit(solution)/shard_map/ppermute | solution.py:271
  9.0 4.0 %collective-permute-start.4 = (bf16[8,2048]{1,0:T(8,128)(2,1)S(1)}, bf16[8,2048]{1,0:T(8,128)(2,1)S(1)}, u32[]{:S(2)}, u32[]{:S(2)}) collective-permute-start(bf16[8,2048]{1,0:T(8,128)(2,1)S(1)} %get-tuple-element.17), channel_id=1, source_target_pairs={{0,2},{1,3},{2,0},{3,1},{4,6},{5,7},{6,4},{7,5},{8,10},{9,11},{10,... | collective-permute-start | bytes 98312 | tf_op jit(solution)/shard_map/ppermute | solution.py:271
  10.0 3.4 %collective-permute-start.5 = (bf16[8,2048]{1,0:T(8,128)(2,1)S(1)}, bf16[8,2048]{1,0:T(8,128)(2,1)S(1)}, u32[]{:S(2)}, u32[]{:S(2)}) collective-permute-start(bf16[8,2048]{1,0:T(8,128)(2,1)S(1)} %get-tuple-element.18), channel_id=1, source_target_pairs={{0,3},{1,2},{2,1},{3,0},{4,7},{5,6},{6,5},{7,4},{8,11},{9,10},{10,... | collective-permute-start | bytes 98312 | tf_op jit(solution)/shard_map/ppermute | solution.py:271
  13.4 4.3 %collective-permute-start.6 = (bf16[8,2048]{1,0:T(8,128)(2,1)S(1)}, bf16[8,2048]{1,0:T(8,128)(2,1)S(1)}, u32[]{:S(2)}, u32[]{:S(2)}) collective-permute-start(bf16[8,2048]{1,0:T(8,128)(2,1)S(1)} %add_zones.1), channel_id=1, source_target_pairs={{0,13},{1,12},{2,15},{3,14},{4,9},{5,8},{6,11},{7,10},{8,5},{9,4},... | collective-permute-start | bytes 98312 | tf_op jit(solution)/shard_map/ppermute | solution.py:281
  15.8 3.4 %collective-permute-start.7 = (bf16[8,2048]{1,0:T(8,128)(2,1)S(1)}, bf16[8,2048]{1,0:T(8,128)(2,1)S(1)}, u32[]{:S(2)}, u32[]{:S(2)}) collective-permute-start(bf16[8,2048]{1,0:T(8,128)(2,1)S(1)} %add_zones.1), channel_id=1, source_target_pairs={{0,9},{1,8},{2,11},{3,10},{4,13},{5,12},{6,15},{7,14},{8,1},{9,0},... | collective-permute-start | bytes 98312 | tf_op jit(solution)/shard_map/ppermute | solution.py:281
  16.2 3.3 %collective-permute-start.8 = (bf16[8,2048]{1,0:T(8,128)(2,1)S(1)}, bf16[8,2048]{1,0:T(8,128)(2,1)S(1)}, u32[]{:S(2)}, u32[]{:S(2)}) collective-permute-start(bf16[8,2048]{1,0:T(8,128)(2,1)S(1)} %add_zones.1), channel_id=1, source_target_pairs={{0,5},{1,4},{2,7},{3,6},{4,1},{5,0},{6,3},{7,2},{8,13},{9,12},{10,... | collective-permute-start | bytes 98312 | tf_op jit(solution)/shard_map/ppermute | solution.py:281
  16.5 3.1 %collective-permute-start.9 = (bf16[8,2048]{1,0:T(8,128)(2,1)S(1)}, bf16[8,2048]{1,0:T(8,128)(2,1)S(1)}, u32[]{:S(2)}, u32[]{:S(2)}) collective-permute-start(bf16[8,2048]{1,0:T(8,128)(2,1)S(1)} %add_zones.1), channel_id=1, source_target_pairs={{0,1},{1,0},{2,3},{3,2},{4,5},{5,4},{6,7},{7,6},{8,9},{9,8},{10,11... | collective-permute-start | bytes 98312 | tf_op jit(solution)/shard_map/ppermute | solution.py:271
  19.7 4.5 %collective-permute-start.11 = (f32[8,2048]{1,0:T(8,128)S(1)}, f32[8,2048]{1,0:T(8,128)S(1)}, u32[]{:S(2)}, u32[]{:S(2)}) collective-permute-start(f32[8,2048]{1,0:T(8,128)S(1)} %get-tuple-element.20), channel_id=1, source_target_pairs={{0,1},{1,0},{2,3},{3,2},{4,5},{5,4},{6,7},{7,6},{8,9},{9,8},{10,11... | collective-permute-start | bytes 196616 | tf_op jit(solution)/shard_map/ppermute | solution.py:271
  19.9 4.2 %collective-permute-start.10 = (bf16[8,2048]{1,0:T(8,128)(2,1)S(1)}, bf16[8,2048]{1,0:T(8,128)(2,1)S(1)}, u32[]{:S(2)}, u32[]{:S(2)}) collective-permute-start(bf16[8,2048]{1,0:T(8,128)(2,1)S(1)} %get-tuple-element.19), channel_id=1, source_target_pairs={{0,17},{1,16},{2,19},{3,18},{4,21},{5,20},{6,23},{7,22},{8,25},{9,... | collective-permute-start | bytes 98312 | tf_op jit(solution)/shard_map/ppermute | solution.py:281

commit v5 on v4

--- a/solution.py
+++ b/solution.py
@@ -237,7 +237,7 @@
     steps = taps.shape[0] // rows
     if steps <= DIRECT:
         outs = [
-            jax.ShapeDtypeStruct((rows, cells), jnp.bfloat16 if step else jnp.float32)
+            jax.ShapeDtypeStruct((rows, cells), jnp.bfloat16)
             for step in range(steps)
         ]
     else:

time: 25 us -> 24.8 us (level)
  no operation moved by 1% of the time
where the time goes in v5:
time: 24.8 us; the launch traced here: 24.6 us
  starting transfers between devices  11.1 us (45%)
  waiting for transfers between devices  7.53 us (30%)
  Pallas kernels  4.91 us (20%)
  other arithmetic  0.95 us (4%)
    ppermute x8, starting transfers between devices, swap(): lax.ppermute(value, axis, [(i, i ^ by) for i in range(lax.axis_size(axis))])  5.68 us
    ppermute x4, starting transfers between devices, swap_both(): return lax.ppermute(value, ('tm', 'zone'), pairs)  5.47 us
    ppermute x4, waiting for transfers between devices, swap_both(): return lax.ppermute(value, ('tm', 'zone'), pairs)  4.25 us
    ppermute x8, waiting for transfers between devices, swap(): lax.ppermute(value, axis, [(i, i ^ by) for i in range(lax.axis_size(axis))])  3.28 us
    pallas_call x1, Pallas kernels, hold(): pl.pallas_call(hold_kernel, out_shape=[jax.ShapeDtypeStruct((count, *weig...  2.23 us
    pallas_call x1, Pallas kernels, remap(): pl.pallas_call(functools.partial(remap_kernel, zones), out_shape=outs, in...  1.65 us
    convert_element_type x1, other arithmetic, shards(): xlow = source_field.astype(jnp.bfloat16)  0.87 us
    pallas_call x1, Pallas kernels, add_up(): pl.pallas_call(sum_kernel, out_shape=jax.ShapeDtypeStruct(parts[0].shape,...  0.64 us
  transfers between devices with their start and end apart: 12, of which 7 were waited for; matrix products, arithmetic and copies ran while one was open for 0% of the time, Pallas kernels for 10%

profile of v5, /device:TPU:0, one launch (start us, length us, event | category | flops | bytes accessed | tf_op | source)
XLA Modules:
  0.0 24.6 jit_solution(5631682413927707680)
XLA Ops:
  0.0 0.9 %convert_element_type.3.refs_0_ = bf16[8,2048]{1,0:T(8,128)(2,1)S(1)} convert(f32[8,2048]{1,0:T(8,128)} %param.5) | non-fusion elementwise | flops 16384 | bytes 98304 | tf_op jit(solution)/shard_map/convert_element_type | solution.py:290
  0.9 2.4 %collective-permute-start = (bf16[8,2048]{1,0:T(8,128)(2,1)S(1)}, bf16[8,2048]{1,0:T(8,128)(2,1)S(1)}, u32[]{:S(2)}, u32[]{:S(2)}) collective-permute-start(bf16[8,2048]{1,0:T(8,128)(2,1)S(1)} %convert_element_type.3.refs_0_), channel_id=1, source_target_pairs={{0,3},{1,2},{2,1},{3,0},{4,7},{5,6},{6,5},{7,4},{8,11},{9,10},{10,... | collective-permute-start | bytes 98312 | tf_op jit(solution)/shard_map/ppermute | solution.py:271
  3.3 0.6 %collective-permute-start.1 = (bf16[8,2048]{1,0:T(8,128)(2,1)S(1)}, bf16[8,2048]{1,0:T(8,128)(2,1)S(1)}, u32[]{:S(2)}, u32[]{:S(2)}) collective-permute-start(bf16[8,2048]{1,0:T(8,128)(2,1)S(1)} %convert_element_type.3.refs_0_), channel_id=1, source_target_pairs={{0,2},{1,3},{2,0},{3,1},{4,6},{5,7},{6,4},{7,5},{8,10},{9,11},{10,... | collective-permute-start | bytes 98312 | tf_op jit(solution)/shard_map/ppermute | solution.py:271
  3.8 0.1 collective-permute-start.2
  4.0 2.2 %hold.1 = (bf16[16,8,128,128]{3,2,1,0:T(8,128)(2,1)S(1)}, bf16[12,8,128,128]{3,2,1,0:T(8,128)(2,1)S(1)}) custom-call(bf16[16,8,128,128]{3,2,1,0:T(8,128)(2,1)} %weights_ref.1), custom_call_target="tpu_custom_call" | custom-call | bytes 8388608 | tf_op jit(solution)/shard_map/hold/pallas_call | solution.py:43
  6.3 1.0 %collective-permute-done.1.refs_2_ = bf16[8,2048]{1,0:T(8,128)(2,1)S(1)} collective-permute-done((bf16[8,2048]{1,0:T(8,128)(2,1)S(1)}, bf16[8,2048]{1,0:T(8,128)(2,1)S(1)}, u32[]{:S(2)}, u32[]{:S(2)}) %collective-permute-start.1) | collective-permute-done | bytes 32800 | tf_op jit(solution)/shard_map/ppermute | solution.py:271
  7.2 1.6 %remap.1 = (f32[8,2048]{1,0:T(8,128)S(1)}, bf16[8,2048]{1,0:T(8,128)(2,1)S(1)}, bf16[8,2048]{1,0:T(8,128)(2,1)S(1)}, bf16[8,2048]{1,0:T(8,128)(2,1)S(1)}) custom-call(s32[1,2]{1,0:T(1,128)S(1)} %add_bitcast_fusion.where_ref, s32[8,16]{1,0:T(8,128)S(1)} %bitcast.6, s32[1,8]{1,0:T(1,128)S(1)} %copy-done.2, bf16[8,2048]{1,0:T(8,128)(2,1)S(1)} %convert_element_type.3.refs_0_, ...), custom_call_target="tpu_custom_call" | custom-call | flops 100000000 | bytes 8388608 | tf_op jit(solution)/shard_map/remap/pallas_call | solution.py:186
  9.0 1.1 %collective-permute-start.4 = (bf16[8,2048]{1,0:T(8,128)(2,1)S(1)}, bf16[8,2048]{1,0:T(8,128)(2,1)S(1)}, u32[]{:S(2)}, u32[]{:S(2)}) collective-permute-start(bf16[8,2048]{1,0:T(8,128)(2,1)S(1)} %get-tuple-element.17), channel_id=1, source_target_pairs={{0,2},{1,3},{2,0},{3,1},{4,6},{5,7},{6,4},{7,5},{8,10},{9,11},{10,... | collective-permute-start | bytes 98312 | tf_op jit(solution)/shard_map/ppermute | solution.py:271
  10.0 0.8 %collective-permute-start.5 = (bf16[8,2048]{1,0:T(8,128)(2,1)S(1)}, bf16[8,2048]{1,0:T(8,128)(2,1)S(1)}, u32[]{:S(2)}, u32[]{:S(2)}) collective-permute-start(bf16[8,2048]{1,0:T(8,128)(2,1)S(1)} %get-tuple-element.18), channel_id=1, source_target_pairs={{0,3},{1,2},{2,1},{3,0},{4,7},{5,6},{6,5},{7,4},{8,11},{9,10},{10,... | collective-permute-start | bytes 98312 | tf_op jit(solution)/shard_map/ppermute | solution.py:271
  10.8 0.2 prepare.1.taps_ref
  11.1 1.9 %collective-permute-done.4.refs_2_ = bf16[8,2048]{1,0:T(8,128)(2,1)S(1)} collective-permute-done((bf16[8,2048]{1,0:T(8,128)(2,1)S(1)}, bf16[8,2048]{1,0:T(8,128)(2,1)S(1)}, u32[]{:S(2)}, u32[]{:S(2)}) %collective-permute-start.4) | collective-permute-done | bytes 32800 | tf_op jit(solution)/shard_map/ppermute | solution.py:271
  13.0 0.4 %collective-permute-done.5.refs_3_ = bf16[8,2048]{1,0:T(8,128)(2,1)S(1)} collective-permute-done((bf16[8,2048]{1,0:T(8,128)(2,1)S(1)}, bf16[8,2048]{1,0:T(8,128)(2,1)S(1)}, u32[]{:S(2)}, u32[]{:S(2)}) %collective-permute-start.5) | collective-permute-done | bytes 32800 | tf_op jit(solution)/shard_map/ppermute | solution.py:271
  13.4 2.4 %collective-permute-start.6 = (bf16[8,2048]{1,0:T(8,128)(2,1)S(1)}, bf16[8,2048]{1,0:T(8,128)(2,1)S(1)}, u32[]{:S(2)}, u32[]{:S(2)}) collective-permute-start(bf16[8,2048]{1,0:T(8,128)(2,1)S(1)} %add_zones.1), channel_id=1, source_target_pairs={{0,13},{1,12},{2,15},{3,14},{4,9},{5,8},{6,11},{7,10},{8,5},{9,4},... | collective-permute-start | bytes 98312 | tf_op jit(solution)/shard_map/ppermute | solution.py:281
  15.8 0.4 %collective-permute-start.7 = (bf16[8,2048]{1,0:T(8,128)(2,1)S(1)}, bf16[8,2048]{1,0:T(8,128)(2,1)S(1)}, u32[]{:S(2)}, u32[]{:S(2)}) collective-permute-start(bf16[8,2048]{1,0:T(8,128)(2,1)S(1)} %add_zones.1), channel_id=1, source_target_pairs={{0,9},{1,8},{2,11},{3,10},{4,13},{5,12},{6,15},{7,14},{8,1},{9,0},... | collective-permute-start | bytes 98312 | tf_op jit(solution)/shard_map/ppermute | solution.py:281
  16.2 0.3 %collective-permute-start.8 = (bf16[8,2048]{1,0:T(8,128)(2,1)S(1)}, bf16[8,2048]{1,0:T(8,128)(2,1)S(1)}, u32[]{:S(2)}, u32[]{:S(2)}) collective-permute-start(bf16[8,2048]{1,0:T(8,128)(2,1)S(1)} %add_zones.1), channel_id=1, source_target_pairs={{0,5},{1,4},{2,7},{3,6},{4,1},{5,0},{6,3},{7,2},{8,13},{9,12},{10,... | collective-permute-start | bytes 98312 | tf_op jit(solution)/shard_map/ppermute | solution.py:281
  16.5 0.3 %collective-permute-start.9 = (bf16[8,2048]{1,0:T(8,128)(2,1)S(1)}, bf16[8,2048]{1,0:T(8,128)(2,1)S(1)}, u32[]{:S(2)}, u32[]{:S(2)}) collective-permute-start(bf16[8,2048]{1,0:T(8,128)(2,1)S(1)} %add_zones.1), channel_id=1, source_target_pairs={{0,1},{1,0},{2,3},{3,2},{4,5},{5,4},{6,7},{7,6},{8,9},{9,8},{10,11... | collective-permute-start | bytes 98312 | tf_op jit(solution)/shard_map/ppermute | solution.py:271
  16.8 0.9 %collective-permute-done.6.refs_0_ = bf16[8,2048]{1,0:T(8,128)(2,1)S(1)} collective-permute-done((bf16[8,2048]{1,0:T(8,128)(2,1)S(1)}, bf16[8,2048]{1,0:T(8,128)(2,1)S(1)}, u32[]{:S(2)}, u32[]{:S(2)}) %collective-permute-start.6) | collective-permute-done | bytes 32800 | tf_op jit(solution)/shard_map/ppermute | solution.py:281
  17.7 1.4 %collective-permute-done.7.refs_1_ = bf16[8,2048]{1,0:T(8,128)(2,1)S(1)} collective-permute-done((bf16[8,2048]{1,0:T(8,128)(2,1)S(1)}, bf16[8,2048]{1,0:T(8,128)(2,1)S(1)}, u32[]{:S(2)}, u32[]{:S(2)}) %collective-permute-start.7) | collective-permute-done | bytes 32800 | tf_op jit(solution)/shard_map/ppermute | solution.py:281
  19.1 0.4 %collective-permute-done.8.refs_2_ = bf16[8,2048]{1,0:T(8,128)(2,1)S(1)} collective-permute-done((bf16[8,2048]{1,0:T(8,128)(2,1)S(1)}, bf16[8,2048]{1,0:T(8,128)(2,1)S(1)}, u32[]{:S(2)}, u32[]{:S(2)}) %collective-permute-start.8) | collective-permute-done | bytes 32800 | tf_op jit(solution)/shard_map/ppermute | solution.py:281
  19.5 0.1 time_filter.1
  19.7 2.4 %collective-permute-start.10 = (bf16[8,2048]{1,0:T(8,128)(2,1)S(1)}, bf16[8,2048]{1,0:T(8,128)(2,1)S(1)}, u32[]{:S(2)}, u32[]{:S(2)}) collective-permute-start(bf16[8,2048]{1,0:T(8,128)(2,1)S(1)} %get-tuple-element.19), channel_id=1, source_target_pairs={{0,17},{1,16},{2,19},{3,18},{4,21},{5,20},{6,23},{7,22},{8,25},{9,... | collective-permute-start | bytes 98312 | tf_op jit(solution)/shard_map/ppermute | solution.py:281
  22.1 0.3 %collective-permute-start.11 = (bf16[8,2048]{1,0:T(8,128)(2,1)S(1)}, bf16[8,2048]{1,0:T(8,128)(2,1)S(1)}, u32[]{:S(2)}, u32[]{:S(2)}) collective-permute-start(bf16[8,2048]{1,0:T(8,128)(2,1)S(1)} %get-tuple-element.20), channel_id=1, source_target_pairs={{0,1},{1,0},{2,3},{3,2},{4,5},{5,4},{6,7},{7,6},{8,9},{9,8},{10,11... | collective-permute-start | bytes 98312 | tf_op jit(solution)/shard_map/ppermute | solution.py:271
  22.5 1.5 %collective-permute-done.10.refs_0_ = bf16[8,2048]{1,0:T(8,128)(2,1)S(1)} collective-permute-done((bf16[8,2048]{1,0:T(8,128)(2,1)S(1)}, bf16[8,2048]{1,0:T(8,128)(2,1)S(1)}, u32[]{:S(2)}, u32[]{:S(2)}) %collective-permute-start.10) | collective-permute-done | bytes 32800 | tf_op jit(solution)/shard_map/ppermute | solution.py:281
  24.0 0.6 %add_up.1 = f32[8,2048]{1,0:T(8,128)} custom-call(bf16[8,2048]{1,0:T(8,128)(2,1)S(1)} %collective-permute-done.10.refs_0_, bf16[8,2048]{1,0:T(8,128)(2,1)S(1)} %collective-permute-done.11.refs_1_), custom_call_target="tpu_custom_call" | custom-call | tf_op jit(solution)/shard_map/add_up/pallas_call | solution.py:260
  (14 shorter events, 0.2 us)
Async XLA Ops:
  0.0 7.2 %copy-start = (s32[16,8]{0,1:T(8,128)S(1)}, s32[16,8]{0,1:T(8,128)}, u32[]{:S(2)}) copy-start(s32[16,8]{0,1:T(8,128)} %param.7) | copy-start | bytes 1540
  0.0 7.2 %copy-start.2 = (s32[1,8]{1,0:T(1,128)S(1)}, s32[1,8]{1,0:T(1,128)}, u32[]{:S(2)}) copy-start(s32[1,8]{1,0:T(1,128)} %sizes_ref.1) | copy-start | bytes 100
  0.9 5.4 %collective-permute-start = (bf16[8,2048]{1,0:T(8,128)(2,1)S(1)}, bf16[8,2048]{1,0:T(8,128)(2,1)S(1)}, u32[]{:S(2)}, u32[]{:S(2)}) collective-permute-start(bf16[8,2048]{1,0:T(8,128)(2,1)S(1)} %convert_element_type.3.refs_0_), channel_id=1, source_target_pairs={{0,3},{1,2},{2,1},{3,0},{4,7},{5,6},{6,5},{7,4},{8,11},{9,10},{10,... | collective-permute-start | bytes 98312 | tf_op jit(solution)/shard_map/ppermute | solution.py:271
  3.3 4.0 %collective-permute-start.1 = (bf16[8,2048]{1,0:T(8,128)(2,1)S(1)}, bf16[8,2048]{1,0:T(8,128)(2,1)S(1)}, u32[]{:S(2)}, u32[]{:S(2)}) collective-permute-start(bf16[8,2048]{1,0:T(8,128)(2,1)S(1)} %convert_element_type.3.refs_0_), channel_id=1, source_target_pairs={{0,2},{1,3},{2,0},{3,1},{4,6},{5,7},{6,4},{7,5},{8,10},{9,11},{10,... | collective-permute-start | bytes 98312 | tf_op jit(solution)/shard_map/ppermute | solution.py:271
  3.8 3.4 %collective-permute-start.2 = (bf16[8,2048]{1,0:T(8,128)(2,1)S(1)}, bf16[8,2048]{1,0:T(8,128)(2,1)S(1)}, u32[]{:S(2)}, u32[]{:S(2)}) collective-permute-start(bf16[8,2048]{1,0:T(8,128)(2,1)S(1)} %convert_element_type.3.refs_0_), channel_id=1, source_target_pairs={{0,1},{1,0},{2,3},{3,2},{4,5},{5,4},{6,7},{7,6},{8,9},{9,8},{10,11... | collective-permute-start | bytes 98312 | tf_op jit(solution)/shard_map/ppermute | solution.py:271
  6.3 4.6 %copy-start.1 = (f32[1023]{0:T(1024)S(1)}, f32[1023]{0:T(1024)}, u32[]{:S(2)}) copy-start(f32[1023]{0:T(1024)} %param.9) | copy-start | bytes 12280
  8.9 2.2 %collective-permute-start.3 = (bf16[8,2048]{1,0:T(8,128)(2,1)S(1)}, bf16[8,2048]{1,0:T(8,128)(2,1)S(1)}, u32[]{:S(2)}, u32[]{:S(2)}) collective-permute-start(bf16[8,2048]{1,0:T(8,128)(2,1)S(1)} %get-tuple-element.16), channel_id=1, source_target_pairs={{0,1},{1,0},{2,3},{3,2},{4,5},{5,4},{6,7},{7,6},{8,9},{9,8},{10,11... | collective-permute-start | bytes 98312 | tf_op jit(solution)/shard_map/ppermute | solution.py:271
  9.0 4.0 %collective-permute-start.4 = (bf16[8,2048]{1,0:T(8,128)(2,1)S(1)}, bf16[8,2048]{1,0:T(8,128)(2,1)S(1)}, u32[]{:S(2)}, u32[]{:S(2)}) collective-permute-start(bf16[8,2048]{1,0:T(8,128)(2,1)S(1)} %get-tuple-element.17), channel_id=1, source_target_pairs={{0,2},{1,3},{2,0},{3,1},{4,6},{5,7},{6,4},{7,5},{8,10},{9,11},{10,... | collective-permute-start | bytes 98312 | tf_op jit(solution)/shard_map/ppermute | solution.py:271
  10.0 3.4 %collective-permute-start.5 = (bf16[8,2048]{1,0:T(8,128)(2,1)S(1)}, bf16[8,2048]{1,0:T(8,128)(2,1)S(1)}, u32[]{:S(2)}, u32[]{:S(2)}) collective-permute-start(bf16[8,2048]{1,0:T(8,128)(2,1)S(1)} %get-tuple-element.18), channel_id=1, source_target_pairs={{0,3},{1,2},{2,1},{3,0},{4,7},{5,6},{6,5},{7,4},{8,11},{9,10},{10,... | collective-permute-start | bytes 98312 | tf_op jit(solution)/shard_map/ppermute | solution.py:271
  13.4 4.3 %collective-permute-start.6 = (bf16[8,2048]{1,0:T(8,128)(2,1)S(1)}, bf16[8,2048]{1,0:T(8,128)(2,1)S(1)}, u32[]{:S(2)}, u32[]{:S(2)}) collective-permute-start(bf16[8,2048]{1,0:T(8,128)(2,1)S(1)} %add_zones.1), channel_id=1, source_target_pairs={{0,13},{1,12},{2,15},{3,14},{4,9},{5,8},{6,11},{7,10},{8,5},{9,4},... | collective-permute-start | bytes 98312 | tf_op jit(solution)/shard_map/ppermute | solution.py:281
  15.8 3.4 %collective-permute-start.7 = (bf16[8,2048]{1,0:T(8,128)(2,1)S(1)}, bf16[8,2048]{1,0:T(8,128)(2,1)S(1)}, u32[]{:S(2)}, u32[]{:S(2)}) collective-permute-start(bf16[8,2048]{1,0:T(8,128)(2,1)S(1)} %add_zones.1), channel_id=1, source_target_pairs={{0,9},{1,8},{2,11},{3,10},{4,13},{5,12},{6,15},{7,14},{8,1},{9,0},... | collective-permute-start | bytes 98312 | tf_op jit(solution)/shard_map/ppermute | solution.py:281
  16.2 3.3 %collective-permute-start.8 = (bf16[8,2048]{1,0:T(8,128)(2,1)S(1)}, bf16[8,2048]{1,0:T(8,128)(2,1)S(1)}, u32[]{:S(2)}, u32[]{:S(2)}) collective-permute-start(bf16[8,2048]{1,0:T(8,128)(2,1)S(1)} %add_zones.1), channel_id=1, source_target_pairs={{0,5},{1,4},{2,7},{3,6},{4,1},{5,0},{6,3},{7,2},{8,13},{9,12},{10,... | collective-permute-start | bytes 98312 | tf_op jit(solution)/shard_map/ppermute | solution.py:281
  16.5 3.1 %collective-permute-start.9 = (bf16[8,2048]{1,0:T(8,128)(2,1)S(1)}, bf16[8,2048]{1,0:T(8,128)(2,1)S(1)}, u32[]{:S(2)}, u32[]{:S(2)}) collective-permute-start(bf16[8,2048]{1,0:T(8,128)(2,1)S(1)} %add_zones.1), channel_id=1, source_target_pairs={{0,1},{1,0},{2,3},{3,2},{4,5},{5,4},{6,7},{7,6},{8,9},{9,8},{10,11... | collective-permute-start | bytes 98312 | tf_op jit(solution)/shard_map/ppermute | solution.py:271
  19.7 4.3 %collective-permute-start.10 = (bf16[8,2048]{1,0:T(8,128)(2,1)S(1)}, bf16[8,2048]{1,0:T(8,128)(2,1)S(1)}, u32[]{:S(2)}, u32[]{:S(2)}) collective-permute-start(bf16[8,2048]{1,0:T(8,128)(2,1)S(1)} %get-tuple-element.19), channel_id=1, source_target_pairs={{0,17},{1,16},{2,19},{3,18},{4,21},{5,20},{6,23},{7,22},{8,25},{9,... | collective-permute-start | bytes 98312 | tf_op jit(solution)/shard_map/ppermute | solution.py:281
  22.1 1.9 %collective-permute-start.11 = (bf16[8,2048]{1,0:T(8,128)(2,1)S(1)}, bf16[8,2048]{1,0:T(8,128)(2,1)S(1)}, u32[]{:S(2)}, u32[]{:S(2)}) collective-permute-start(bf16[8,2048]{1,0:T(8,128)(2,1)S(1)} %get-tuple-element.20), channel_id=1, source_target_pairs={{0,1},{1,0},{2,3},{3,2},{4,5},{5,4},{6,7},{7,6},{8,9},{9,8},{10,11... | collective-permute-start | bytes 98312 | tf_op jit(solution)/shard_map/ppermute | solution.py:271
